TPU v7x, 256 devices: a whole 4x4x8 slice. The times are simulated.
256 devices in a mesh: ctx: 64 (over x, z_lo, y, core), head: 4 (over z_hi).
Axes of the slice: x: 4, y: 4, z: 8 (z_hi: 4, z_lo: 2; z = z_hi * 2 + z_lo), core: 2. Of those that a mesh axis runs over, the one named last changes fastest.
Arguments:
- layer_input: bfloat16 [8192, 8192], P('ctx'), may hold values from -6 to 6
- key_weight: bfloat16 [8192, 512], P(None, 'head'), may hold values from -0.0625 to 0.0625
- value_weight: bfloat16 [8192, 512], P(None, 'head'), may hold values from -0.0625 to 0.0625
- queries: bfloat16 [8192, 4096], P('ctx', 'head'), may hold values from -160 to 160
- out_grad: bfloat16 [8192, 4096], P('ctx', 'head'), may hold values from -192 to 192
- doc_start: int32 [8192], P('ctx'), may hold values from 0 to 8191, as said below
- block_order: int32 [128], replicated, may hold values from 0 to 127, as said below
Outputs:
- input_grad: bfloat16 [8192, 8192], P('ctx', 'head')
- query_grad: bfloat16 [8192, 4096], P('ctx', 'head')
Inputs may be any that keep to these rules, and one draw needn't show every extreme that they name: `block_order`: entries 2d and 2d + 1 are j and 127 - j for some j < 64; all entries together are a permutation. doc_start of a row is the first position of the row's document, at most the row's own position; documents are runs of positions, at most 8 of them, and the last position forms a document of its own.
All inputs are finite; a program needn't handle non-finite values.
Results may differ from a plain program's by a relative error of at most 0.018.
Values may be sent and summed in bfloat16 or wider, within the bound.
No kernel may reach another device: no remote copies, remote signals or barrier semaphores. Data moves between devices by JAX's collectives and lax.ppermute only.
A program may use at most 128 MiB of HBM per device.

v0:
```python
import math

import jax
import jax.numpy as jnp
from jax import lax
from jax.sharding import PartitionSpec as P

rope_base = 500000.0
big_negative = -1e30


def rotation_tables(positions, width):
    half_width = width // 2
    exponent = jnp.arange(half_width, dtype=jnp.float32) * (2.0 / width)
    frequency = jnp.exp(-math.log(rope_base) * exponent)
    angles = positions.astype(jnp.float32)[:, None] * frequency[None, :]
    return (jnp.cos(angles), jnp.sin(angles))


def rotate(vectors, cos_table, sin_table):
    half_width = vectors.shape[1] // 2
    first_half = vectors[:, :half_width]
    second_half = vectors[:, half_width:]
    return jnp.concatenate(
        [
            first_half * cos_table - second_half * sin_table,
            second_half * cos_table + first_half * sin_table,
        ],
        axis=1,
    )


def unrotate(vectors, cos_table, sin_table):
    half_width = vectors.shape[1] // 2
    first_half = vectors[:, :half_width]
    second_half = vectors[:, half_width:]
    return jnp.concatenate(
        [
            first_half * cos_table + second_half * sin_table,
            second_half * cos_table - first_half * sin_table,
        ],
        axis=1,
    )


def block_positions(sequence_blocks, block_len):
    offsets = jnp.arange(block_len, dtype=jnp.int32)
    return (sequence_blocks[:, None] * block_len + offsets[None, :]).reshape(-1)


def shards(layer_input, key_weight, value_weight, queries, out_grad, doc_start, block_order):
    row_count = layer_input.shape[0]
    block_len = row_count // 2
    head_dim = key_weight.shape[1]
    groups = queries.shape[1] // head_dim
    scaling = 1.0 / math.sqrt(head_dim)
    highest = lax.Precision.HIGHEST
    device = lax.axis_index("ctx")
    own_pos = block_positions(lax.dynamic_slice_in_dim(block_order, 2 * device, 2), block_len)
    all_pos = block_positions(block_order, block_len)
    cos_own, sin_own = rotation_tables(own_pos, head_dim)
    key_raw = jnp.dot(layer_input, key_weight, preferred_element_type=jnp.float32)
    keys_local = rotate(key_raw, cos_own, sin_own)
    values_local = jnp.dot(layer_input, value_weight, preferred_element_type=jnp.float32).astype(
        jnp.bfloat16
    )
    all_keys = lax.all_gather(keys_local, "ctx", axis=0, tiled=True)
    all_values = lax.all_gather(values_local, "ctx", axis=0, tiled=True)
    total_keys = all_keys.shape[0]
    key_span = 512
    tile_count = total_keys // key_span
    query_tiles = queries.reshape(row_count, groups, head_dim)
    query_wide = query_tiles.astype(jnp.float32)
    grad_tiles = out_grad.reshape(row_count, groups, head_dim)
    key_blocks = (
        all_keys.reshape(tile_count, key_span, head_dim),
        all_values.reshape(tile_count, key_span, head_dim),
        all_pos.reshape(tile_count, key_span),
    )

    def live_mask(key_pos):
        return (key_pos[None, :] <= own_pos[:, None]) & (key_pos[None, :] >= doc_start[:, None])

    def scored(key_tile):
        return (
            jnp.einsum(
                "tgd,kd->tgk",
                query_wide,
                key_tile,
                precision=highest,
                preferred_element_type=jnp.float32,
            )
            * scaling
        )

    def stats_step(state_in, block_in):
        key_tile, value_tile, key_pos = block_in
        live_now = live_mask(key_pos)

        def update(carried):
            row_top, row_total, weighted = carried
            live_three = live_now[:, None, :]
            scores_tile = jnp.where(live_three, scored(key_tile), big_negative)
            new_top = jnp.maximum(row_top, jnp.max(scores_tile, axis=-1))
            growth = jnp.where(live_three, jnp.exp(scores_tile - new_top[..., None]), 0.0)
            prob_grad = jnp.einsum(
                "tgd,kd->tgk", grad_tiles, value_tile, preferred_element_type=jnp.float32
            )
            faded = jnp.exp(row_top - new_top)
            return (
                new_top,
                row_total * faded + jnp.sum(growth, axis=-1),
                weighted * faded + jnp.sum(growth * prob_grad, axis=-1),
            )

        def keep_state(carried):
            return carried

        return (lax.cond(jnp.any(live_now), update, keep_state, state_in), None)

    stat_shape = (row_count, groups)
    stats_init = (
        jnp.full(stat_shape, big_negative, jnp.float32),
        jnp.zeros(stat_shape, jnp.float32),
        jnp.zeros(stat_shape, jnp.float32),
    )
    (row_top, row_total, weighted), _ = lax.scan(stats_step, stats_init, key_blocks)
    log_total = row_top + jnp.log(row_total)
    row_delta = weighted / row_total

    def tile_terms(key_tile, value_tile, key_pos):
        live_three = live_mask(key_pos)[:, None, :]
        prob_tile = jnp.where(live_three, jnp.exp(scored(key_tile) - log_total[..., None]), 0.0)
        prob_grad = jnp.einsum(
            "tgd,kd->tgk", grad_tiles, value_tile, preferred_element_type=jnp.float32
        )
        score_grad = (prob_tile * (prob_grad - row_delta[..., None]) * scaling).astype(jnp.bfloat16)
        return (prob_tile.astype(jnp.bfloat16), score_grad)

    def tile_grads(probs_half, score_grad):
        key_term = jnp.einsum(
            "tgk,tgd->kd", score_grad, query_tiles, preferred_element_type=jnp.float32
        )
        value_term = jnp.einsum(
            "tgk,tgd->kd", probs_half, grad_tiles, preferred_element_type=jnp.float32
        )
        return jnp.concatenate([key_term, value_term], axis=1)

    def query_term(score_grad, key_tile):
        return jnp.einsum(
            "tgk,kd->tgd",
            score_grad.astype(jnp.float32),
            key_tile,
            precision=highest,
            preferred_element_type=jnp.float32,
        )

    query_init = jnp.zeros((row_count, groups, head_dim), jnp.float32)

    def grad_step(accumulated, block_in):
        key_tile, value_tile, key_pos = block_in

        def compute_tile(running):
            probs_half, score_grad = tile_terms(key_tile, value_tile, key_pos)
            return (running + query_term(score_grad, key_tile), tile_grads(probs_half, score_grad))

        def skip_tile(running):
            return (running, jnp.zeros((key_pos.shape[0], 2 * head_dim), jnp.float32))

        return lax.cond(jnp.any(live_mask(key_pos)), compute_tile, skip_tile, accumulated)

    query_acc, kv_terms = lax.scan(grad_step, query_init, key_blocks)
    summed_grads = lax.psum_scatter(
        kv_terms.reshape(total_keys, 2 * head_dim), "ctx", scatter_dimension=0, tiled=True
    )
    query_grad = query_acc.reshape(row_count, groups * head_dim).astype(jnp.bfloat16)
    key_back = unrotate(summed_grads[:, :head_dim], cos_own, sin_own).astype(jnp.bfloat16)
    value_back = summed_grads[:, head_dim:].astype(jnp.bfloat16)
    contract = (((1,), (1,)), ((), ()))
    partial_sum = lax.dot_general(
        key_back, key_weight, contract, preferred_element_type=jnp.float32
    )
    partial_sum = partial_sum + lax.dot_general(
        value_back, value_weight, contract, preferred_element_type=jnp.float32
    )
    input_grad = lax.psum_scatter(partial_sum, "head", scatter_dimension=1, tiled=True).astype(
        jnp.bfloat16
    )
    return (input_grad, query_grad)


def solution(mesh):
    return jax.shard_map(
        shards,
        mesh=mesh,
        in_specs=(
            P("ctx", None),
            P(None, "head"),
            P(None, "head"),
            P("ctx", "head"),
            P("ctx", "head"),
            P("ctx"),
            P(),
        ),
        out_specs=(P("ctx", "head"), P("ctx", "head")),
        check_vma=False,
    )
```

profile of v0, /device:TPU:1, one launch (start us, length us, event | category | flops | bytes accessed | tf_op | source)
XLA Modules:
  0.0 1137.5 jit_solution(14185709924599179899)
XLA Ops:
  17.0 116.9 %all-gather.3.cloned.1.call-done = f32[8192,128]{0,1:T(8,128)} async-done(((f32[128,128]{0,1:T(8,128)}), f32[8192,128]{0,1:T(8,128)}) %all-gather.3.cloned.1.call-update) | async-done | bytes 4194320 | tf_op jit(solution)/shard_map/all_gather | solution.py:67
  139.5 100.9 %all-gather.5.cloned.1.call-done = bf16[8192,128]{1,0:T(8,128)(2,1)} async-done(((bf16[128,128]{1,0:T(8,128)(2,1)}), bf16[8192,128]{1,0:T(8,128)(2,1)}) %all-gather.5.cloned.1.call-update) | async-done | bytes 2097168 | tf_op jit(solution)/shard_map/all_gather | solution.py:68
  240.4 106.7 %while.31 = (s32[]{:T(128)}, f32[128,8]{0,1:T(8,128)S(1)}, f32[128,8]{0,1:T(8,128)S(1)}, f32[128,8]{0,1:T(8,128)S(1)}, s32[16,512]{1,0:T(8,128)S(1)}, /*index=5*...) while((s32[]{:T(128)}, f32[128,8]{0,1:T(8,128)S(1)}, ...), condition=%wide.region_7.8_spmd.clone, body=%wide.region_0.7_spmd.clone.sunk | while | flops 947129472 | bytes 7816975 | solution.py:127
  348.0 381.6 %while.32 = (s32[]{:T(128)}, f32[128,8,128]{2,0,1:T(8,128)}, f32[16,512,256]{1,0,2:T(8,128)}, s32[16,512]{1,0:T(8,128)S(1)}, s32[128]{0:T(128)S(1)}, /*index=5*/...) while((s32[]{:T(128)}, f32[128,8,128]{2,0,1:T(8,128)}, ...), condition=%wide.region_12.13_spmd.clone, body=%wide.region_8.12_spmd.clone.sunk | while | flops 2018181248 | bytes 23615884 | solution.py:172
  349.7 8.2 conditional.7
  360.3 11.5 %dynamic_update_slice.6 = f32[16,512,256]{1,0,2:T(8,128)} dynamic-update-slice(f32[16,512,256]{1,0,2:T(8,128)} %get-tuple-element.730, f32[1,512,256]{1,0,2:T(1,128)S(1)} %copy.59, s32[]{:T(128)} %copy.86, s32[]{:T(128)} %constant.81.clone.1..sunk, s32[]{:T(128)} %constant.81.clone.1..sunk) | dynamic-update-slice | bytes 1048580 | tf_op jit(solution)/shard_map/while/body/jit(dynamic_update_index_in_dim)/dynamic_update_slice | solution.py:172
  384.1 11.5 %dynamic_update_slice.6 = f32[16,512,256]{1,0,2:T(8,128)} dynamic-update-slice(f32[16,512,256]{1,0,2:T(8,128)} %get-tuple-element.730, f32[1,512,256]{1,0,2:T(1,128)S(1)} %copy.59, s32[]{:T(128)} %copy.86, s32[]{:T(128)} %constant.81.clone.1..sunk, s32[]{:T(128)} %constant.81.clone.1..sunk) | dynamic-update-slice | bytes 1048580 | tf_op jit(solution)/shard_map/while/body/jit(dynamic_update_index_in_dim)/dynamic_update_slice | solution.py:172
  397.4 8.2 conditional.7
  408.0 11.5 %dynamic_update_slice.6 = f32[16,512,256]{1,0,2:T(8,128)} dynamic-update-slice(f32[16,512,256]{1,0,2:T(8,128)} %get-tuple-element.730, f32[1,512,256]{1,0,2:T(1,128)S(1)} %copy.59, s32[]{:T(128)} %copy.86, s32[]{:T(128)} %constant.81.clone.1..sunk, s32[]{:T(128)} %constant.81.clone.1..sunk) | dynamic-update-slice | bytes 1048580 | tf_op jit(solution)/shard_map/while/body/jit(dynamic_update_index_in_dim)/dynamic_update_slice | solution.py:172
  431.8 11.5 %dynamic_update_slice.6 = f32[16,512,256]{1,0,2:T(8,128)} dynamic-update-slice(f32[16,512,256]{1,0,2:T(8,128)} %get-tuple-element.730, f32[1,512,256]{1,0,2:T(1,128)S(1)} %copy.59, s32[]{:T(128)} %copy.86, s32[]{:T(128)} %constant.81.clone.1..sunk, s32[]{:T(128)} %constant.81.clone.1..sunk) | dynamic-update-slice | bytes 1048580 | tf_op jit(solution)/shard_map/while/body/jit(dynamic_update_index_in_dim)/dynamic_update_slice | solution.py:172
  445.0 8.2 conditional.7
  455.6 11.5 %dynamic_update_slice.6 = f32[16,512,256]{1,0,2:T(8,128)} dynamic-update-slice(f32[16,512,256]{1,0,2:T(8,128)} %get-tuple-element.730, f32[1,512,256]{1,0,2:T(1,128)S(1)} %copy.59, s32[]{:T(128)} %copy.86, s32[]{:T(128)} %constant.81.clone.1..sunk, s32[]{:T(128)} %constant.81.clone.1..sunk) | dynamic-update-slice | bytes 1048580 | tf_op jit(solution)/shard_map/while/body/jit(dynamic_update_index_in_dim)/dynamic_update_slice | solution.py:172
  479.5 11.5 %dynamic_update_slice.6 = f32[16,512,256]{1,0,2:T(8,128)} dynamic-update-slice(f32[16,512,256]{1,0,2:T(8,128)} %get-tuple-element.730, f32[1,512,256]{1,0,2:T(1,128)S(1)} %copy.59, s32[]{:T(128)} %copy.86, s32[]{:T(128)} %constant.81.clone.1..sunk, s32[]{:T(128)} %constant.81.clone.1..sunk) | dynamic-update-slice | bytes 1048580 | tf_op jit(solution)/shard_map/while/body/jit(dynamic_update_index_in_dim)/dynamic_update_slice | solution.py:172
  492.7 8.2 conditional.7
  503.3 11.5 %dynamic_update_slice.6 = f32[16,512,256]{1,0,2:T(8,128)} dynamic-update-slice(f32[16,512,256]{1,0,2:T(8,128)} %get-tuple-element.730, f32[1,512,256]{1,0,2:T(1,128)S(1)} %copy.59, s32[]{:T(128)} %copy.86, s32[]{:T(128)} %constant.81.clone.1..sunk, s32[]{:T(128)} %constant.81.clone.1..sunk) | dynamic-update-slice | bytes 1048580 | tf_op jit(solution)/shard_map/while/body/jit(dynamic_update_index_in_dim)/dynamic_update_slice | solution.py:172
  527.2 11.5 %dynamic_update_slice.6 = f32[16,512,256]{1,0,2:T(8,128)} dynamic-update-slice(f32[16,512,256]{1,0,2:T(8,128)} %get-tuple-element.730, f32[1,512,256]{1,0,2:T(1,128)S(1)} %copy.59, s32[]{:T(128)} %copy.86, s32[]{:T(128)} %constant.81.clone.1..sunk, s32[]{:T(128)} %constant.81.clone.1..sunk) | dynamic-update-slice | bytes 1048580 | tf_op jit(solution)/shard_map/while/body/jit(dynamic_update_index_in_dim)/dynamic_update_slice | solution.py:172
  540.4 8.2 conditional.7
  551.0 11.5 %dynamic_update_slice.6 = f32[16,512,256]{1,0,2:T(8,128)} dynamic-update-slice(f32[16,512,256]{1,0,2:T(8,128)} %get-tuple-element.730, f32[1,512,256]{1,0,2:T(1,128)S(1)} %copy.59, s32[]{:T(128)} %copy.86, s32[]{:T(128)} %constant.81.clone.1..sunk, s32[]{:T(128)} %constant.81.clone.1..sunk) | dynamic-update-slice | bytes 1048580 | tf_op jit(solution)/shard_map/while/body/jit(dynamic_update_index_in_dim)/dynamic_update_slice | solution.py:172
  564.3 8.2 conditional.7
  574.9 11.5 %dynamic_update_slice.6 = f32[16,512,256]{1,0,2:T(8,128)} dynamic-update-slice(f32[16,512,256]{1,0,2:T(8,128)} %get-tuple-element.730, f32[1,512,256]{1,0,2:T(1,128)S(1)} %copy.59, s32[]{:T(128)} %copy.86, s32[]{:T(128)} %constant.81.clone.1..sunk, s32[]{:T(128)} %constant.81.clone.1..sunk) | dynamic-update-slice | bytes 1048580 | tf_op jit(solution)/shard_map/while/body/jit(dynamic_update_index_in_dim)/dynamic_update_slice | solution.py:172
  598.7 11.5 %dynamic_update_slice.6 = f32[16,512,256]{1,0,2:T(8,128)} dynamic-update-slice(f32[16,512,256]{1,0,2:T(8,128)} %get-tuple-element.730, f32[1,512,256]{1,0,2:T(1,128)S(1)} %copy.59, s32[]{:T(128)} %copy.86, s32[]{:T(128)} %constant.81.clone.1..sunk, s32[]{:T(128)} %constant.81.clone.1..sunk) | dynamic-update-slice | bytes 1048580 | tf_op jit(solution)/shard_map/while/body/jit(dynamic_update_index_in_dim)/dynamic_update_slice | solution.py:172
  622.6 11.5 %dynamic_update_slice.6 = f32[16,512,256]{1,0,2:T(8,128)} dynamic-update-slice(f32[16,512,256]{1,0,2:T(8,128)} %get-tuple-element.730, f32[1,512,256]{1,0,2:T(1,128)S(1)} %copy.59, s32[]{:T(128)} %copy.86, s32[]{:T(128)} %constant.81.clone.1..sunk, s32[]{:T(128)} %constant.81.clone.1..sunk) | dynamic-update-slice | bytes 1048580 | tf_op jit(solution)/shard_map/while/body/jit(dynamic_update_index_in_dim)/dynamic_update_slice | solution.py:172
  646.4 11.5 %dynamic_update_slice.6 = f32[16,512,256]{1,0,2:T(8,128)} dynamic-update-slice(f32[16,512,256]{1,0,2:T(8,128)} %get-tuple-element.730, f32[1,512,256]{1,0,2:T(1,128)S(1)} %copy.59, s32[]{:T(128)} %copy.86, s32[]{:T(128)} %constant.81.clone.1..sunk, s32[]{:T(128)} %constant.81.clone.1..sunk) | dynamic-update-slice | bytes 1048580 | tf_op jit(solution)/shard_map/while/body/jit(dynamic_update_index_in_dim)/dynamic_update_slice | solution.py:172
  659.7 8.2 conditional.7
  670.3 11.5 %dynamic_update_slice.6 = f32[16,512,256]{1,0,2:T(8,128)} dynamic-update-slice(f32[16,512,256]{1,0,2:T(8,128)} %get-tuple-element.730, f32[1,512,256]{1,0,2:T(1,128)S(1)} %copy.59, s32[]{:T(128)} %copy.86, s32[]{:T(128)} %constant.81.clone.1..sunk, s32[]{:T(128)} %constant.81.clone.1..sunk) | dynamic-update-slice | bytes 1048580 | tf_op jit(solution)/shard_map/while/body/jit(dynamic_update_index_in_dim)/dynamic_update_slice | solution.py:172
  683.5 8.2 conditional.7
  694.1 11.5 %dynamic_update_slice.6 = f32[16,512,256]{1,0,2:T(8,128)} dynamic-update-slice(f32[16,512,256]{1,0,2:T(8,128)} %get-tuple-element.730, f32[1,512,256]{1,0,2:T(1,128)S(1)} %copy.59, s32[]{:T(128)} %copy.86, s32[]{:T(128)} %constant.81.clone.1..sunk, s32[]{:T(128)} %constant.81.clone.1..sunk) | dynamic-update-slice | bytes 1048580 | tf_op jit(solution)/shard_map/while/body/jit(dynamic_update_index_in_dim)/dynamic_update_slice | solution.py:172
  707.4 8.2 conditional.7
  718.0 11.5 %dynamic_update_slice.6 = f32[16,512,256]{1,0,2:T(8,128)} dynamic-update-slice(f32[16,512,256]{1,0,2:T(8,128)} %get-tuple-element.730, f32[1,512,256]{1,0,2:T(1,128)S(1)} %copy.59, s32[]{:T(128)} %copy.86, s32[]{:T(128)} %constant.81.clone.1..sunk, s32[]{:T(128)} %constant.81.clone.1..sunk) | dynamic-update-slice | bytes 1048580 | tf_op jit(solution)/shard_map/while/body/jit(dynamic_update_index_in_dim)/dynamic_update_slice | solution.py:172
  729.5 14.6 %copy.56 = f32[32,8,16,512]{3,1,2,0:T(8,128)} copy(f32[32,8,16,512]{3,2,1,0:T(8,128)} %bitcast.87) | data formatting | bytes 16777216
  744.2 293.5 %reduce-scatter.3.cloned.1.call-done = f32[128,256]{0,1:T(8,128)} async-done(((f32[8192,256]{0,1:T(8,128)}), f32[128,256]{0,1:T(8,128)}) %reduce-scatter.3.cloned.1.call-update) | async-done | bytes 131088 | tf_op jit(solution)/shard_map/reduce_scatter | solution.py:173
  1044.8 84.1 %reduce-scatter.5.cloned.1.call-done = f32[128,2048]{1,0:T(8,128)} async-done(((f32[128,8192]{1,0:T(8,128)}), f32[128,2048]{1,0:T(8,128)}) %reduce-scatter.5.cloned.1.call-update) | async-done | bytes 1048592 | tf_op jit(solution)/shard_map/reduce_scatter | solution.py:186
  (576 shorter events, 445.2 us)
Async XLA Ops:
  7.2 1.6 copy-start
  7.2 126.7 %all-gather.3.cloned.1.call-start = ((), (), s32[]{:S(2)}) async-start(), calls=%async_computation.2 | async-start | bytes 4259840 | tf_op jit(solution)/shard_map/all_gather | solution.py:67
  12.2 3.8 copy-start.12
  12.2 4.1 copy-start.8
  12.2 4.2 copy-start.9
  12.2 228.2 %all-gather.5.cloned.1.call-start = ((), (), s32[]{:S(2)}) async-start(), calls=%async_computation.3 | async-start | bytes 2129920 | tf_op jit(solution)/shard_map/all_gather | solution.py:68
  15.9 1021.9 %reduce-scatter.3.cloned.1.call-start = ((), (), s32[]{:S(2)}) async-start(), calls=%async_computation.4 | async-start | bytes 8519680 | tf_op jit(solution)/shard_map/reduce_scatter | solution.py:173
  16.4 123.1 %copy-start.5 = (bf16[128,1024]{0,1:T(8,128)(2,1)}, bf16[128,1024]{0,1:T(8,128)(2,1)S(1)}, u32[]{:S(2)}) copy-start(bf16[128,1024]{0,1:T(8,128)(2,1)S(1)} %copy.39) | copy-start | bytes 786436
  17.0 223.4 %copy-start.11 = (s32[128]{0:T(128)S(1)}, s32[128]{0:T(128)}, u32[]{:S(2)}) copy-start(s32[128]{0:T(128)} %param.20) | copy-start | bytes 1540
  353.0 1.4 copy-start.2
  354.4 2.9 copy-start.6
  376.8 1.4 copy-start.2
  378.2 2.9 copy-start.6
  400.7 1.4 copy-start.2
  402.1 2.9 copy-start.6
  424.5 1.4 copy-start.2
  425.9 2.9 copy-start.6
  449.8 2.9 copy-start.6
  473.6 2.9 copy-start.6
  497.4 2.9 copy-start.6
  521.3 2.9 copy-start.6
  545.1 2.9 copy-start.6
  569.0 2.9 copy-start.6
  592.8 2.9 copy-start.6
  616.7 2.9 copy-start.6
  640.6 2.9 copy-start.6
  664.4 2.9 copy-start.6
  688.3 2.9 copy-start.6
  712.1 2.9 copy-start.6
  744.2 384.7 %reduce-scatter.5.cloned.1.call-start = ((), (), s32[]{:S(2)}) async-start(), calls=%async_computation.5 | async-start | bytes 5242880 | tf_op jit(solution)/shard_map/reduce_scatter | solution.py:186
  1038.7 1.6 copy-start.7
  1038.7 1.6 copy-start.10
  (45 other events, 47.2 us)
Sparse Core Ops, SparseCore 0:
  12.3 121.5 all-gather.2
  135.8 104.5 all-gather.4
  744.3 293.3 reduce-scatter.2
  1043.1 85.6 reduce-scatter.4
where the time goes:
time: 1150 us; the launch traced here: 1140 us
  waiting for transfers between devices  595 us (52%)
  local copies, waits for them, and re-layouts  252 us (22%)
  matrix products  207 us (18%)
  other arithmetic  45.1 us (4%)
  loops' own time  23.8 us (2%)
  between operations  13.9 us (1%)
    reduce_scatter x1, waiting for transfers between devices, shards(): lax.psum_scatter(kv_terms.reshape(total_keys, 2 * head_dim), 'ctx', scatt...  293 us
    dynamic_update_slice x32, local copies, waits for them, and re-layouts, shards(): query_acc, kv_terms = lax.scan(grad_step, query_init, key_blocks)  210 us
    all_gather x1, waiting for transfers between devices, shards(): all_keys = lax.all_gather(keys_local, 'ctx', axis=0, tiled=True)  117 us
    all_gather x1, waiting for transfers between devices, shards(): all_values = lax.all_gather(values_local, 'ctx', axis=0, tiled=True)  101 us
    dot_general x32, matrix products, scored(): jnp.einsum('tgd,kd->tgk', query_wide, key_tile, precision=highest, prefer...  95.6 us
    reduce_scatter x1, waiting for transfers between devices, shards(): lax.psum_scatter(partial_sum, 'head', scatter_dimension=1, tiled=True)  84.1 us
    dot_general x16, matrix products, query_term(): jnp.einsum('tgk,kd->tgd', score_grad.astype(jnp.float32), key_tile, preci...  38.3 us
    dot_general x16, matrix products, update(): jnp.einsum('tgd,kd->tgk', grad_tiles, value_tile, preferred_element_type=...  26.3 us
  transfers between devices with their start and end apart: 4, of which 4 were waited for; matrix products, arithmetic and copies ran while one was open for 1% of the time, Pallas kernels for 0%

commit v1 on v0

v1 whole, which is shorter than its diff:
```python
import functools
import math

import jax
import jax.numpy as jnp
from jax import lax
from jax.experimental import pallas as pl
from jax.experimental.pallas import tpu as pltpu
from jax.sharding import PartitionSpec as P

rope_base = 500000.0
big_negative = -1e30
n_ctx = 64
n_head = 4
block_len = 64
key_span = 256
log2e = 1.4426950408889634


def split_index(c):
    return c // 16, (c // 8) % 2, (c // 2) % 4, c % 2


def join_index(x, z, y, core):
    return ((x * 2 + z) * 4 + y) * 2 + core


def make_perm(target):
    return [(c, join_index(*target(*split_index(c)))) for c in range(n_ctx)]


core_perm = make_perm(lambda x, z, y, k: (x, z, y, 1 - k))
z_perm = make_perm(lambda x, z, y, k: (x, 1 - z, y, k))


def first_perm(s):
    return make_perm(
        lambda x, z, y, k: ((x + s) % 4, z, y, k) if k == 0 else (x, z, (y + s) % 4, k)
    )


def second_perm(s):
    return make_perm(
        lambda x, z, y, k: (x, z, (y + s) % 4, k) if k == 0 else ((x + s) % 4, z, y, k)
    )


def head_perm(s):
    return [(h, (h + s) % n_head) for h in range(n_head)]


def rotation_tables(positions, width):
    half_width = width // 2
    exponent = jnp.arange(half_width, dtype=jnp.float32) * (2.0 / width)
    frequency = jnp.exp(-math.log(rope_base) * exponent)
    angles = positions.astype(jnp.float32)[:, None] * frequency[None, :]
    return (jnp.cos(angles), jnp.sin(angles))


def rotate(vectors, cos_table, sin_table):
    half_width = vectors.shape[1] // 2
    a = vectors[:, :half_width]
    b = vectors[:, half_width:]
    return jnp.concatenate([a * cos_table - b * sin_table, b * cos_table + a * sin_table], axis=1)


def unrotate(vectors, cos_table, sin_table):
    return rotate(vectors, cos_table, -sin_table)


def attention_kernel(
    place_ref,
    order_ref,
    *refs,
    scaling,
    tokens,
):
    pieces = refs[:8]
    qt_ref, dot_ref, q_ref, do_ref, pos_ref, start_ref = refs[8:14]
    outs = refs[14:22]
    dqt_ref = refs[22]
    kv, acc, dq_acc, sem = refs[23:]
    x, z, y, core = place_ref[0], place_ref[1], place_ref[2], place_ref[3]

    def sequence_block(piece, i):
        s2 = piece % 4
        holder = core if piece < 4 else 1 - core
        s1 = i // 4
        src_z = jnp.where((i // 2) % 2 == 0, z, 1 - z)
        src_core = jnp.where(i % 2 == 0, holder, 1 - holder)
        dx = jnp.where(holder == 0, s1, s2)
        dy = jnp.where(holder == 0, s2, s1)
        src_x = (x + 4 - dx) % 4
        src_y = (y + 4 - dy) % 4
        stored = (((src_x * 2 + src_z) * 4 + src_y) * 2 + src_core) * 2 + holder
        return order_ref[stored]

    for piece in range(8):

        def fetch(i, carry, piece=piece):
            seq = sequence_block(piece, i)
            pltpu.make_async_copy(
                pieces[piece].at[pl.ds(pl.multiple_of(i * block_len, block_len), block_len), :],
                kv.at[pl.ds(pl.multiple_of(seq * block_len, block_len), block_len), :],
                sem,
            ).start()
            return carry

        lax.fori_loop(0, 16, fetch, 0)

    acc[...] = jnp.zeros_like(acc)
    pltpu.make_async_copy(kv, kv, sem).wait()

    half = q_ref.shape[0] // 2
    head_dim = q_ref.shape[1]
    factor = scaling * log2e
    for part in range(2):
        cols = pl.ds(part * half, half)
        own_block = place_ref[4 + part]
        first = place_ref[6 + part] // key_span
        last = own_block * block_len // key_span + 1
        pos = pos_ref[:, cols]
        start = start_ref[:, cols]

        def tile(kt):
            rows = pl.ds(pl.multiple_of(kt * key_span, key_span), key_span)
            key = kv[rows, : 2 * head_dim]
            value = kv[rows, 2 * head_dim :]
            score = (
                jnp.dot(key, qt_ref[:, cols], preferred_element_type=jnp.float32) * factor
            )
            prob_grad = jnp.dot(value, dot_ref[:, cols], preferred_element_type=jnp.float32)
            key_pos = kt * key_span + lax.broadcasted_iota(jnp.int32, (key_span, half), 0)
            live = (key_pos <= pos) & (key_pos >= start)
            return rows, key, score, prob_grad, live

        def stats(kt, carried):
            top, total, weighted = carried
            _, _, score, prob_grad, live = tile(kt)
            score = jnp.where(live, score, big_negative)
            new_top = jnp.maximum(top, jnp.max(score, axis=0, keepdims=True))
            growth = jnp.exp2(score - new_top)
            faded = jnp.exp2(top - new_top)
            return (
                new_top,
                total * faded + jnp.sum(growth, axis=0, keepdims=True),
                weighted * faded + jnp.sum(growth * prob_grad, axis=0, keepdims=True),
            )

        row = (1, half)
        top, total, weighted = lax.fori_loop(
            first,
            last,
            stats,
            (
                jnp.full(row, big_negative, jnp.float32),
                jnp.zeros(row, jnp.float32),
                jnp.zeros(row, jnp.float32),
            ),
        )
        log_total = top + jnp.log2(total)
        delta = weighted / total
        dq_acc[...] = jnp.zeros_like(dq_acc)

        def grads(kt, carry):
            rows, key, score, prob_grad, live = tile(kt)
            prob = jnp.where(live, jnp.exp2(score - log_total), 0.0)
            score_grad = (prob * (prob_grad - delta) * scaling).astype(jnp.bfloat16)
            acc[rows, :head_dim] += jnp.dot(
                score_grad, q_ref[cols, :], preferred_element_type=jnp.float32
            )
            acc[rows, head_dim:] += jnp.dot(
                prob.astype(jnp.bfloat16), do_ref[cols, :], preferred_element_type=jnp.float32
            )
            dq_acc[...] += jnp.dot(key.T, score_grad, preferred_element_type=jnp.float32)
            return carry

        lax.fori_loop(first, last, grads, 0)
        dqt_ref[:, cols] = dq_acc[:head_dim, :] + dq_acc[head_dim:, :]

    for piece in range(8):

        def store(i, carry, piece=piece):
            seq = sequence_block(piece, i)
            outs[piece][pl.ds(pl.multiple_of(i * block_len, block_len), block_len), :] = acc[
                pl.ds(pl.multiple_of(seq * block_len, block_len), block_len), :
            ].astype(jnp.bfloat16)
            return carry

        lax.fori_loop(0, 16, store, 0)


def attention(place, order, pieces, qt, dot_, q, do, pos, start, scaling, tokens):
    head_dim = q.shape[1]
    rows = q.shape[0]
    smem = pl.BlockSpec(memory_space=pltpu.SMEM)
    vmem = pl.BlockSpec(memory_space=pltpu.VMEM)
    piece_rows = tokens // 8
    return pl.pallas_call(
        functools.partial(attention_kernel, scaling=scaling, tokens=tokens),
        out_shape=[jax.ShapeDtypeStruct((piece_rows, 2 * head_dim), jnp.bfloat16)] * 8
        + [jax.ShapeDtypeStruct((head_dim, rows), jnp.float32)],
        in_specs=[smem, smem] + [pl.BlockSpec(memory_space=pl.ANY)] * 8 + [vmem] * 6,
        out_specs=[vmem] * 9,
        scratch_shapes=[
            pltpu.VMEM((tokens, 3 * head_dim), jnp.bfloat16),
            pltpu.VMEM((tokens, 2 * head_dim), jnp.float32),
            pltpu.VMEM((2 * head_dim, rows // 2), jnp.float32),
            pltpu.SemaphoreType.DMA,
        ],
        compiler_params=pltpu.CompilerParams(vmem_limit_bytes=48 * 1024 * 1024),
        cost_estimate=pl.CostEstimate(
            flops=10 * rows * tokens * head_dim,
            bytes_accessed=12 * 1024 * 1024,
            transcendentals=rows * tokens,
        ),
    )(place, order, *pieces, qt, dot_, q, do, pos, start)


def shards(layer_input, key_weight, value_weight, queries, out_grad, doc_start, block_order):
    f32, bf16 = jnp.float32, jnp.bfloat16
    row_count = layer_input.shape[0]
    tokens = row_count * n_ctx
    head_dim = key_weight.shape[1]
    width = key_weight.shape[0]
    groups = queries.shape[1] // head_dim
    scaling = 1.0 / math.sqrt(head_dim)
    device = lax.axis_index("ctx")
    head = lax.axis_index("head")
    x, z, y, core = split_index(device)
    own_blocks = lax.dynamic_slice_in_dim(block_order, 2 * device, 2)
    own_pos = (
        own_blocks[:, None] * block_len + jnp.arange(block_len, dtype=jnp.int32)[None, :]
    ).reshape(-1)
    cos_own, sin_own = rotation_tables(own_pos, head_dim)

    def send(v, perm):
        return lax.ppermute(v, "ctx", perm)

    key_raw = jnp.dot(layer_input, key_weight, preferred_element_type=f32)
    keys = rotate(key_raw, cos_own, sin_own)
    key_hi = lax.reduce_precision(keys, 8, 7)
    key_lo = keys - key_hi
    values = jnp.dot(layer_input, value_weight, preferred_element_type=f32)
    local = jnp.concatenate(
        [key_hi.astype(bf16), key_lo.astype(bf16), values.astype(bf16)], axis=1
    ).reshape(2, block_len, 3 * head_dim)

    kept = lax.dynamic_index_in_dim(local, core, 0, keepdims=False)
    given = lax.dynamic_index_in_dim(local, 1 - core, 0, keepdims=False)
    pair = jnp.concatenate([kept, send(given, core_perm)], axis=0)
    node = jnp.concatenate([pair, send(pair, z_perm)], axis=0)
    line = jnp.concatenate([node] + [send(node, first_perm(s)) for s in (1, 2, 3)], axis=0)
    mine = [line] + [send(line, second_perm(s)) for s in (1, 2, 3)]
    others = [send(v, core_perm) for v in mine]

    out_width = width // n_head
    half_width = out_width // 2
    both_weights = jnp.concatenate([key_weight, value_weight], axis=1).reshape(
        n_head, 2, half_width, 2 * head_dim
    )

    def weight_part(to_head, part):
        return lax.dynamic_slice(
            both_weights, (to_head, part, 0, 0), (1, 1, half_width, 2 * head_dim)
        )[0, 0]

    core_is_zero = core == 0
    weights = [lax.dynamic_index_in_dim(both_weights, head, 0, keepdims=False)]
    for s in (1, 2, 3):
        half_own = lax.ppermute(weight_part((head + s) % n_head, core), "head", head_perm(s))
        half_other = send(half_own, core_perm)
        weights.append(
            jnp.where(
                core_is_zero,
                jnp.stack([half_own, half_other]),
                jnp.stack([half_other, half_own]),
            )
        )

    def by_block(v):
        return v.reshape(2, block_len, groups, head_dim)

    q_blocks = by_block(queries)
    g_blocks = by_block(out_grad)
    rows = row_count * groups
    q_rows = q_blocks.transpose(0, 2, 1, 3).reshape(rows, head_dim)
    g_rows = g_blocks.transpose(0, 2, 1, 3).reshape(rows, head_dim)
    q_cols = q_blocks.transpose(3, 0, 2, 1).reshape(head_dim, rows)
    g_cols = g_blocks.transpose(3, 0, 2, 1).reshape(head_dim, rows)
    q_cols = jnp.concatenate([q_cols, q_cols], axis=0)

    def per_column(v):
        return jnp.broadcast_to(v.reshape(2, 1, block_len), (2, groups, block_len)).reshape(1, rows)

    starts = doc_start.reshape(2, block_len)[:, 0]
    place = jnp.concatenate([jnp.stack([x, z, y, core]), own_blocks, starts]).astype(jnp.int32)
    result = attention(
        place,
        block_order,
        mine + others,
        q_cols,
        g_cols,
        q_rows,
        g_rows,
        per_column(own_pos),
        per_column(doc_start),
        scaling,
        tokens,
    )
    parts, dq_cols = result[:8], result[8]
    query_grad = (
        dq_cols.reshape(head_dim, 2, groups, block_len)
        .transpose(1, 3, 2, 0)
        .reshape(row_count, groups * head_dim)
        .astype(bf16)
    )

    def added(*terms):
        total = terms[0].astype(f32)
        for term in terms[1:]:
            total = total + term.astype(f32)
        return total

    merged = [added(parts[s], send(parts[4 + s], core_perm)).astype(bf16) for s in range(4)]
    line_grad = added(merged[0], *[send(merged[s], second_perm(4 - s)) for s in (1, 2, 3)])
    line_grad = line_grad.astype(bf16).reshape(4, 4 * block_len, 2 * head_dim)
    node_grad = added(line_grad[0], *[send(line_grad[s], first_perm(4 - s)) for s in (1, 2, 3)])
    node_grad = node_grad.astype(bf16).reshape(2, 2 * block_len, 2 * head_dim)
    pair_grad = added(node_grad[0], send(node_grad[1], z_perm)).reshape(
        2, block_len, 2 * head_dim
    )
    other_grad = send(pair_grad[1].astype(bf16), core_perm).astype(f32)
    summed = jnp.where(
        core_is_zero,
        jnp.concatenate([pair_grad[0], other_grad]),
        jnp.concatenate([other_grad, pair_grad[0]]),
    )
    key_back = unrotate(summed[:, :head_dim], cos_own, sin_own).astype(bf16)
    back = jnp.concatenate([key_back, summed[:, head_dim:].astype(bf16)], axis=1)
    backs = [back] + [lax.ppermute(back, "head", head_perm(s)) for s in (1, 2, 3)]
    contract = (((1,), (1,)), ((), ()))
    total = jnp.zeros((row_count, out_width), f32)
    for b, w in zip(backs, weights):
        total = total + lax.dot_general(
            b, w.reshape(out_width, 2 * head_dim), contract, preferred_element_type=f32
        )
    return (total.astype(bf16), query_grad)


def solution(mesh):
    return jax.shard_map(
        shards,
        mesh=mesh,
        in_specs=(
            P("ctx", None),
            P(None, "head"),
            P(None, "head"),
            P("ctx", "head"),
            P("ctx", "head"),
            P("ctx"),
            P(),
        ),
        out_specs=(P("ctx", "head"), P("ctx", "head")),
        check_vma=False,
    )
```

time: 1150 us -> 198 us (0.17)
  waiting for transfers between devices: 595 us -> 41.5 us
  local copies, waits for them, and re-layouts: 252 us -> 22.1 us
  matrix products: 207 us -> 5.82 us
  starting transfers between devices: 0.16 us -> 79.9 us
  other arithmetic: 45.1 us -> 18.2 us
  Pallas kernels: 0 us -> 26.5 us
  loops' own time: 23.8 us -> 0 us
  between operations: 13.9 us -> 1.1 us
    reduce_scatter x2 -> x0, waiting for transfers between devices: 378 us -> none  [the longest x1 293 us: shards(): lax.psum_scatter(kv_terms.reshape(total_keys, 2 * head_dim), 'ctx', scatt...]
    all_gather x2 -> x0, waiting for transfers between devices: 218 us -> none  [the longest x1 117 us: shards(): all_keys = lax.all_gather(keys_local, 'ctx', axis=0, tiled=True)]
    dynamic_update_slice x32 -> x0, local copies, waits for them, and re-layouts: 210 us -> none  [shards(): query_acc, kv_terms = lax.scan(grad_step, query_init, key_blocks)]
    dot_general x116 -> x6, matrix products: 207 us -> 5.82 us  [the longest x4 2.69 us: shards(): lax.dot_general(b, w.reshape(out_width, 2 * head_dim), contract, preferre...]
    ppermute x0 -> x33, starting transfers between devices: none -> 79.9 us  [the longest x27 59.3 us: send(): return lax.ppermute(v, 'ctx', perm)]
    ppermute x0 -> x33, waiting for transfers between devices: none -> 41.5 us  [the longest x27 26.9 us: send(): return lax.ppermute(v, 'ctx', perm)]
    pallas_call x0 -> x1, Pallas kernels: none -> 26.5 us  [attention(): pl.pallas_call(functools.partial(attention_kernel, scaling=scaling, token...]
    another operation x34 -> x0, loops' own time: 23.8 us -> none  [the longest x1 11.5 us: shards(): query_acc, kv_terms = lax.scan(grad_step, query_init, key_blocks)]
  transfers between devices with their start and end apart: 4 -> 33, of which waited for: 4 -> 10; matrix products, arithmetic and copies ran while one was open for 1% -> 17% of each run, Pallas kernels for 0% -> 0%
where the time goes in v1:
time: 198 us; the launch traced here: 195 us
  starting transfers between devices  79.9 us (40%)
  waiting for transfers between devices  41.5 us (21%)
  Pallas kernels  26.5 us (13%)
  local copies, waits for them, and re-layouts  22.1 us (11%)
  other arithmetic  18.2 us (9%)
  matrix products  5.82 us (3%)
    ppermute x27, starting transfers between devices, send(): return lax.ppermute(v, 'ctx', perm)  59.3 us
    ppermute x27, waiting for transfers between devices, send(): return lax.ppermute(v, 'ctx', perm)  26.9 us
    pallas_call x1, Pallas kernels, attention(): pl.pallas_call(functools.partial(attention_kernel, scaling=scaling, token...  26.5 us
    ppermute x3, waiting for transfers between devices, shards(): lax.ppermute(weight_part((head + s) % n_head, core), 'head', head_perm(s))  13.1 us
    ppermute x3, starting transfers between devices, shards(): lax.ppermute(back, 'head', head_perm(s))  11.2 us
    unnamed x50, local copies, waits for them, and re-layouts  9.84 us
    ppermute x3, starting transfers between devices, shards(): lax.ppermute(weight_part((head + s) % n_head, core), 'head', head_perm(s))  9.35 us
    select_n x3, other arithmetic, shards(): jnp.where(core_is_zero, jnp.stack([half_own, half_other]), jnp.stack([hal...  6.4 us
  transfers between devices with their start and end apart: 33, of which 10 were waited for; matrix products, arithmetic and copies ran while one was open for 17% of the time, Pallas kernels for 0%

profile of v1, /device:TPU:1, one launch (start us, length us, event | category | flops | bytes accessed | tf_op | source)
XLA Modules:
  0.0 195.1 jit_solution(15059175827680368508)
XLA Ops:
  2.2 2.4 %fusion.20 = f32[128,128]{1,0:T(8,128)S(1)} fusion(bf16[128,8192]{1,0:T(8,128)(2,1)S(1)} %copy-done, bf16[8192,128]{1,0:T(8,128)(2,1)} %param.8), kind=kOutput, calls=%fused_computation.68 | convolution fusion | flops 268435456 | bytes 4259840 | tf_op jit(solution)/shard_map/dot_general | solution.py:240
  5.9 3.3 %collective-permute-start = (bf16[64,384]{1,0:T(8,128)(2,1)S(1)}, bf16[64,384]{1,0:T(8,128)(2,1)S(1)}, u32[]{:S(2)}, u32[]{:S(2)}) collective-permute-start(bf16[64,384]{1,0:T(8,128)(2,1)S(1)} %dynamic-slice_bitcast_fusion.3), channel_id=1, source_target_pairs={{0,4},{4,0},{8,12},{12,8},{16,20},{20,16},{24,28},{28,24},{32,36},... | collective-permute-start | bytes 147464 | tf_op jit(solution)/shard_map/ppermute | solution.py:238
  10.2 4.0 %collective-permute-done.1 = bf16[128,384]{1,0:T(8,128)(2,1)S(1)} collective-permute-done((bf16[128,384]{1,0:T(8,128)(2,1)S(1)}, bf16[128,384]{1,0:T(8,128)(2,1)S(1)}, u32[]{:S(2)}, u32[]{:S(2)}) %collective-permute-start.1) | collective-permute-done | bytes 98336 | tf_op jit(solution)/shard_map/ppermute | solution.py:238
  15.0 2.5 %collective-permute-start.3 = (bf16[256,384]{1,0:T(8,128)(2,1)S(1)}, bf16[256,384]{1,0:T(8,128)(2,1)S(1)}, u32[]{:S(2)}, u32[]{:S(2)}) collective-permute-start(bf16[256,384]{1,0:T(8,128)(2,1)S(1)} %pad_maximum_fusion.2), channel_id=1, source_target_pairs={{0,128},{4,20},{8,136},{12,28},{16,144},{20,4},{24,152},{28,12},{3... | collective-permute-start | bytes 589832 | tf_op jit(solution)/shard_map/ppermute | solution.py:238
  19.3 3.2 %collective-permute-done.2 = bf16[256,384]{1,0:T(8,128)(2,1)S(1)} collective-permute-done((bf16[256,384]{1,0:T(8,128)(2,1)S(1)}, bf16[256,384]{1,0:T(8,128)(2,1)S(1)}, u32[]{:S(2)}, u32[]{:S(2)}) %collective-permute-start.2) | collective-permute-done | bytes 196640 | tf_op jit(solution)/shard_map/ppermute | solution.py:238
  27.7 2.9 %collective-permute-start.8 = (bf16[1024,384]{1,0:T(8,128)(2,1)}, bf16[1024,384]{1,0:T(8,128)(2,1)}, u32[]{:S(2)}, u32[]{:S(2)}) collective-permute-start(bf16[1024,384]{1,0:T(8,128)(2,1)} %constant_dynamic-update-slice_fusion.refs_0_), channel_id=1, source_target_pairs={{0,4},{4,0},{8,12},{12,8},{16,20},{20,16},{24,28},{28,24},{32,36},... | collective-permute-start | bytes 2359304 | tf_op jit(solution)/shard_map/ppermute | solution.py:238
  30.6 7.0 %collective-permute-done.6.refs_2_ = bf16[1024,384]{1,0:T(8,128)(2,1)} collective-permute-done((bf16[1024,384]{1,0:T(8,128)(2,1)}, bf16[1024,384]{1,0:T(8,128)(2,1)}, u32[]{:S(2)}, u32[]{:S(2)}) %collective-permute-start.6) | collective-permute-done | bytes 786464 | tf_op jit(solution)/shard_map/ppermute | solution.py:238
  37.6 3.0 %collective-permute-start.10 = (bf16[1024,384]{1,0:T(8,128)(2,1)}, bf16[1024,384]{1,0:T(8,128)(2,1)}, u32[]{:S(2)}, u32[]{:S(2)}) collective-permute-start(bf16[1024,384]{1,0:T(8,128)(2,1)} %collective-permute-done.6.refs_2_), channel_id=1, source_target_pairs={{0,4},{4,0},{8,12},{12,8},{16,20},{20,16},{24,28},{28,24},{32,36},... | collective-permute-start | bytes 2359304 | tf_op jit(solution)/shard_map/ppermute | solution.py:238
  40.6 4.7 %collective-permute-done.7.refs_3_ = bf16[1024,384]{1,0:T(8,128)(2,1)} collective-permute-done((bf16[1024,384]{1,0:T(8,128)(2,1)}, bf16[1024,384]{1,0:T(8,128)(2,1)}, u32[]{:S(2)}, u32[]{:S(2)}) %collective-permute-start.7) | collective-permute-done | bytes 786464 | tf_op jit(solution)/shard_map/ppermute | solution.py:238
  45.3 2.7 %collective-permute-start.11 = (bf16[1024,384]{1,0:T(8,128)(2,1)}, bf16[1024,384]{1,0:T(8,128)(2,1)}, u32[]{:S(2)}, u32[]{:S(2)}) collective-permute-start(bf16[1024,384]{1,0:T(8,128)(2,1)} %collective-permute-done.7.refs_3_), channel_id=1, source_target_pairs={{0,4},{4,0},{8,12},{12,8},{16,20},{20,16},{24,28},{28,24},{32,36},... | collective-permute-start | bytes 2359304 | tf_op jit(solution)/shard_map/ppermute | solution.py:238
  55.3 26.5 %shard_map.86 = (bf16[1024,256]{1,0:T(8,128)(2,1)S(1)}, bf16[1024,256]{1,0:T(8,128)(2,1)S(1)}, bf16[1024,256]{1,0:T(8,128)(2,1)S(1)}, bf16[1024,256]{1,0:T(8,128...) custom-call(s32[8]{0:T(128)S(1)} %concatenate.38.place_ref, ...), custom_call_target="tpu_custom_call" | custom-call | flops 10737418240 | bytes 12582912 | tf_op jit(solution)/shard_map/pallas_call | solution.py:199
  85.5 2.5 %pad_maximum_fusion = bf16[8192,256]{1,0:T(8,128)(2,1)} fusion(bf16[8192,128]{1,0:T(8,128)(2,1)S(1)} %copy-done.13, bf16[8192,128]{1,0:T(8,128)(2,1)S(1)} %copy-done.14), kind=kLoop, calls=%fused_computation | loop fusion | flops 8388608 | bytes 8388608 | tf_op jit(solution)/shard_map/concatenate | solution.py:259
  88.0 2.3 %dynamic-slice_bitcast_fusion.1 = (bf16[1024,256]{1,0:T(8,128)(2,1)}, bf16[1024,256]{1,0:T(8,128)(2,1)S(1)}, bf16[1024,256]{1,0:T(8,128)(2,1)S(1)}) fusion(bf16[4,2,1024,256]{3,2,1,0:T(8,128)(2,1)} %bitcast.73, s32[]{:T(128)S(6)} %select_n.117, s32[]{:T(128)S(6)} %select_n.107, s32[]{:T(128)S(6)} %select_n.121, s32[]{:T(128)S(6)} %select_n.113), kind=kLoop, calls=%fused_computation.16 | loop fusion | bytes 3145744 | tf_op jit(solution)/shard_map/squeeze | solution.py:264
  90.3 2.0 %collective-permute-start.25 = (bf16[1024,256]{1,0:T(8,128)(2,1)S(1)}, bf16[1024,256]{1,0:T(8,128)(2,1)}, u32[]{:S(2)}, u32[]{:S(2)}) collective-permute-start(bf16[1024,256]{1,0:T(8,128)(2,1)S(1)} %get-tuple-element.26), channel_id=1, source_target_pairs={{0,1},{1,2},{2,3},{3,0},{4,5},{5,6},{6,7},{7,4},{8,9},{9,10},{10,1... | collective-permute-start | bytes 1572872 | tf_op jit(solution)/shard_map/ppermute | solution.py:271
  92.4 2.9 %collective-permute-start.31 = (bf16[1024,256]{1,0:T(8,128)(2,1)S(1)}, bf16[1024,256]{1,0:T(8,128)(2,1)}, u32[]{:S(2)}, u32[]{:S(2)}) collective-permute-start(bf16[1024,256]{1,0:T(8,128)(2,1)S(1)} %get-tuple-element.25), channel_id=1, source_target_pairs={{0,3},{1,0},{2,1},{3,2},{4,7},{5,4},{6,5},{7,6},{8,11},{9,8},{10,9... | collective-permute-start | bytes 1572872 | tf_op jit(solution)/shard_map/ppermute | solution.py:271
  95.2 4.5 %collective-permute-start.28 = (bf16[1024,256]{1,0:T(8,128)(2,1)}, bf16[1024,256]{1,0:T(8,128)(2,1)}, u32[]{:S(2)}, u32[]{:S(2)}) collective-permute-start(bf16[1024,256]{1,0:T(8,128)(2,1)} %get-tuple-element.24), channel_id=1, source_target_pairs={{0,2},{1,3},{2,0},{3,1},{4,6},{5,7},{6,4},{7,5},{8,10},{9,11},{10,... | collective-permute-start | bytes 1572872 | tf_op jit(solution)/shard_map/ppermute | solution.py:271
  101.0 2.0 %add_convert_fusion.3 = bf16[1024,256]{1,0:T(8,128)(2,1)} fusion(bf16[1024,256]{1,0:T(8,128)(2,1)} %collective-permute-done.13, bf16[1024,256]{1,0:T(8,128)(2,1)S(1)} %copy-done.2), kind=kLoop, calls=%fused_computation.12 | loop fusion | flops 1048576 | bytes 1572864 | tf_op jit(solution)/shard_map/convert_element_type | solution.py:325
  103.0 2.0 %add_convert_fusion.2 = bf16[1024,256]{1,0:T(8,128)(2,1)} fusion(bf16[1024,256]{1,0:T(8,128)(2,1)} %collective-permute-done.15, bf16[1024,256]{1,0:T(8,128)(2,1)S(1)} %get-tuple-element.15), kind=kLoop, calls=%fused_computation.11 | loop fusion | flops 1048576 | bytes 1572864 | tf_op jit(solution)/shard_map/convert_element_type | solution.py:325
  105.0 11.5 %collective-permute-start.14 = (bf16[1024,256]{1,0:T(8,128)(2,1)}, bf16[1024,256]{1,0:T(8,128)(2,1)}, u32[]{:S(2)}, u32[]{:S(2)}) collective-permute-start(bf16[1024,256]{1,0:T(8,128)(2,1)} %add_convert_fusion.3), channel_id=1, source_target_pairs={{0,24},{4,196},{8,0},{12,204},{16,8},{20,212},{24,16},{28,220},{32... | collective-permute-start | bytes 1572872 | tf_op jit(solution)/shard_map/ppermute | solution.py:238
  118.6 13.1 %collective-permute-done.31 = bf16[1024,256]{1,0:T(8,128)(2,1)} collective-permute-done((bf16[1024,256]{1,0:T(8,128)(2,1)S(1)}, bf16[1024,256]{1,0:T(8,128)(2,1)}, u32[]{:S(2)}, u32[]{:S(2)}) %collective-permute-start.31) | collective-permute-done | bytes 524320 | tf_op jit(solution)/shard_map/ppermute | solution.py:271
  131.7 5.2 %collective-permute-start.18 = (bf16[1024,256]{1,0:T(8,128)(2,1)}, bf16[1024,256]{1,0:T(8,128)(2,1)}, u32[]{:S(2)}, u32[]{:S(2)}) collective-permute-start(bf16[1024,256]{1,0:T(8,128)(2,1)} %add_convert_fusion.1), channel_id=1, source_target_pairs={{0,8},{4,68},{8,16},{12,76},{16,24},{20,84},{24,0},{28,92},{32,40}... | collective-permute-start | bytes 1572872 | tf_op jit(solution)/shard_map/ppermute | solution.py:238
  136.9 2.3 %constant_dynamic-slice_fusion = bf16[1,2,1024,256]{3,2,1,0:T(8,128)(2,1)} fusion(bf16[4,2,1024,256]{3,2,1,0:T(8,128)(2,1)} %bitcast.74, s32[]{:T(128)S(6)} %select_n.110), kind=kLoop, calls=%fused_computation.61 | loop fusion | bytes 2097156 | tf_op jit(solution)/shard_map/jit(dynamic_index_in_dim)/dynamic_slice | solution.py:269
  139.2 6.5 %collective-permute-start.26 = (bf16[1024,256]{1,0:T(8,128)(2,1)}, bf16[1024,256]{1,0:T(8,128)(2,1)S(1)}, u32[]{:S(2)}, u32[]{:S(2)}) collective-permute-start(bf16[1024,256]{1,0:T(8,128)(2,1)} %collective-permute-done.25), channel_id=1, source_target_pairs={{0,4},{4,0},{8,12},{12,8},{16,20},{20,16},{24,28},{28,24},{32,36},... | collective-permute-start | bytes 1572872 | tf_op jit(solution)/shard_map/ppermute | solution.py:238
  146.2 4.0 %collective-permute-done.18 = bf16[1024,256]{1,0:T(8,128)(2,1)} collective-permute-done((bf16[1024,256]{1,0:T(8,128)(2,1)}, bf16[1024,256]{1,0:T(8,128)(2,1)}, u32[]{:S(2)}, u32[]{:S(2)}) %collective-permute-start.18) | collective-permute-done | bytes 524320 | tf_op jit(solution)/shard_map/ppermute | solution.py:238
  152.1 3.2 %collective-permute-start.20 = (bf16[256,256]{1,0:T(8,128)(2,1)S(1)}, bf16[256,256]{1,0:T(8,128)(2,1)S(1)}, u32[]{:S(2)}, u32[]{:S(2)}) collective-permute-start(bf16[256,256]{1,0:T(8,128)(2,1)S(1)} %get-tuple-element.29), channel_id=1, source_target_pairs={{0,128},{4,20},{8,136},{12,28},{16,144},{20,4},{24,152},{28,12},{3... | collective-permute-start | bytes 393224 | tf_op jit(solution)/shard_map/ppermute | solution.py:238
  157.7 2.6 %collective-permute-done.21 = bf16[256,256]{1,0:T(8,128)(2,1)S(1)} collective-permute-done((bf16[256,256]{1,0:T(8,128)(2,1)S(1)}, bf16[256,256]{1,0:T(8,128)(2,1)S(1)}, u32[]{:S(2)}, u32[]{:S(2)}) %collective-permute-start.21) | collective-permute-done | bytes 131104 | tf_op jit(solution)/shard_map/ppermute | solution.py:238
  160.4 6.4 %collective-permute-start.22 = (bf16[128,256]{1,0:T(8,128)(2,1)S(1)}, bf16[128,256]{1,0:T(8,128)(2,1)S(1)}, u32[]{:S(2)}, u32[]{:S(2)}) collective-permute-start(bf16[128,256]{1,0:T(8,128)(2,1)S(1)} %slice.77), channel_id=1, source_target_pairs={{0,32},{4,36},{8,40},{12,44},{16,48},{20,52},{24,56},{28,60},{32,0... | collective-permute-start | bytes 196616 | tf_op jit(solution)/shard_map/ppermute | solution.py:238
  166.8 2.5 %maximum_select_fusion.2 = bf16[2,1024,256]{2,1,0:T(8,128)(2,1)} fusion(bf16[1,1024,256]{2,1,0:T(8,128)(2,1)S(1)} %bitcast.86, bf16[1,1024,256]{2,1,0:T(8,128)(2,1)} %bitcast.26, pred[]{:T(512)S(6)} %eq.10), kind=kLoop, calls=%fused_computation.8 | loop fusion | flops 1572864 | bytes 2097153 | tf_op jit(solution)/shard_map/jit(_where)/select_n | solution.py:274
  169.9 3.2 %collective-permute-start.23 = (bf16[64,256]{1,0:T(8,128)(2,1)}, bf16[64,256]{1,0:T(8,128)(2,1)}, u32[]{:S(2)}, u32[]{:S(2)}) collective-permute-start(bf16[64,256]{1,0:T(8,128)(2,1)} %slice.97), channel_id=1, source_target_pairs={{0,4},{4,0},{8,12},{12,8},{16,20},{20,16},{24,28},{28,24},{32,36},... | collective-permute-start | bytes 98312 | tf_op jit(solution)/shard_map/ppermute | solution.py:238
  173.1 2.5 %maximum_select_fusion.1 = bf16[2,1024,256]{2,1,0:T(8,128)(2,1)} fusion(bf16[1,1024,256]{2,1,0:T(8,128)(2,1)S(1)} %bitcast.85, bf16[1,1024,256]{2,1,0:T(8,128)(2,1)} %bitcast.22, pred[]{:T(512)S(6)} %eq.10), kind=kLoop, calls=%fused_computation.7 | loop fusion | flops 1572864 | bytes 2097153 | tf_op jit(solution)/shard_map/jit(_where)/select_n | solution.py:274
  179.7 6.2 %collective-permute-start.24 = (bf16[128,256]{1,0:T(8,128)(2,1)S(1)}, bf16[128,256]{1,0:T(8,128)(2,1)S(1)}, u32[]{:S(2)}, u32[]{:S(2)}) collective-permute-start(bf16[128,256]{1,0:T(8,128)(2,1)S(1)} %pad_maximum_fusion.6), channel_id=1, source_target_pairs={{0,1},{1,2},{2,3},{3,0},{4,5},{5,6},{6,7},{7,4},{8,9},{9,10},{10,1... | collective-permute-start | bytes 196616 | tf_op jit(solution)/shard_map/ppermute | solution.py:341
  185.9 5.0 %collective-permute-start.27 = (bf16[128,256]{1,0:T(8,128)(2,1)S(1)}, bf16[128,256]{1,0:T(8,128)(2,1)S(1)}, u32[]{:S(2)}, u32[]{:S(2)}) collective-permute-start(bf16[128,256]{1,0:T(8,128)(2,1)S(1)} %pad_maximum_fusion.6), channel_id=1, source_target_pairs={{0,2},{1,3},{2,0},{3,1},{4,6},{5,7},{6,4},{7,5},{8,10},{9,11},{10,... | collective-permute-start | bytes 196616 | tf_op jit(solution)/shard_map/ppermute | solution.py:341
  (142 shorter events, 39.4 us)
Async XLA Ops:
  5.9 4.2 %collective-permute-start = (bf16[64,384]{1,0:T(8,128)(2,1)S(1)}, bf16[64,384]{1,0:T(8,128)(2,1)S(1)}, u32[]{:S(2)}, u32[]{:S(2)}) collective-permute-start(bf16[64,384]{1,0:T(8,128)(2,1)S(1)} %dynamic-slice_bitcast_fusion.3), channel_id=1, source_target_pairs={{0,4},{4,0},{8,12},{12,8},{16,20},{20,16},{24,28},{28,24},{32,36},... | collective-permute-start | bytes 147464 | tf_op jit(solution)/shard_map/ppermute | solution.py:238
  14.3 8.2 %collective-permute-start.2 = (bf16[256,384]{1,0:T(8,128)(2,1)S(1)}, bf16[256,384]{1,0:T(8,128)(2,1)S(1)}, u32[]{:S(2)}, u32[]{:S(2)}) collective-permute-start(bf16[256,384]{1,0:T(8,128)(2,1)S(1)} %pad_maximum_fusion.2), channel_id=1, source_target_pairs={{0,64},{4,12},{8,72},{12,20},{16,80},{20,28},{24,88},{28,4},{32,96... | collective-permute-start | bytes 589832 | tf_op jit(solution)/shard_map/ppermute | solution.py:238
  15.0 8.2 %collective-permute-start.3 = (bf16[256,384]{1,0:T(8,128)(2,1)S(1)}, bf16[256,384]{1,0:T(8,128)(2,1)S(1)}, u32[]{:S(2)}, u32[]{:S(2)}) collective-permute-start(bf16[256,384]{1,0:T(8,128)(2,1)S(1)} %pad_maximum_fusion.2), channel_id=1, source_target_pairs={{0,128},{4,20},{8,136},{12,28},{16,144},{20,4},{24,152},{28,12},{3... | collective-permute-start | bytes 589832 | tf_op jit(solution)/shard_map/ppermute | solution.py:238
  17.5 6.4 %collective-permute-start.4 = (bf16[256,384]{1,0:T(8,128)(2,1)S(1)}, bf16[256,384]{1,0:T(8,128)(2,1)S(1)}, u32[]{:S(2)}, u32[]{:S(2)}) collective-permute-start(bf16[256,384]{1,0:T(8,128)(2,1)S(1)} %pad_maximum_fusion.2), channel_id=1, source_target_pairs={{0,192},{4,28},{8,200},{12,4},{16,208},{20,12},{24,216},{28,20},{3... | collective-permute-start | bytes 589832 | tf_op jit(solution)/shard_map/ppermute | solution.py:238
  24.6 13.0 %collective-permute-start.6 = (bf16[1024,384]{1,0:T(8,128)(2,1)}, bf16[1024,384]{1,0:T(8,128)(2,1)}, u32[]{:S(2)}, u32[]{:S(2)}) collective-permute-start(bf16[1024,384]{1,0:T(8,128)(2,1)} %constant_dynamic-update-slice_fusion.refs_0_), channel_id=1, source_target_pairs={{0,16},{4,132},{8,24},{12,140},{16,0},{20,148},{24,8},{28,156},{32... | collective-permute-start | bytes 2359304 | tf_op jit(solution)/shard_map/ppermute | solution.py:238
  26.3 19.1 %collective-permute-start.7 = (bf16[1024,384]{1,0:T(8,128)(2,1)}, bf16[1024,384]{1,0:T(8,128)(2,1)}, u32[]{:S(2)}, u32[]{:S(2)}) collective-permute-start(bf16[1024,384]{1,0:T(8,128)(2,1)} %constant_dynamic-update-slice_fusion.refs_0_), channel_id=1, source_target_pairs={{0,24},{4,196},{8,0},{12,204},{16,8},{20,212},{24,16},{28,220},{32... | collective-permute-start | bytes 2359304 | tf_op jit(solution)/shard_map/ppermute | solution.py:238
  27.1 20.9 %collective-permute-start.5 = (bf16[1024,384]{1,0:T(8,128)(2,1)}, bf16[1024,384]{1,0:T(8,128)(2,1)}, u32[]{:S(2)}, u32[]{:S(2)}) collective-permute-start(bf16[1024,384]{1,0:T(8,128)(2,1)} %constant_dynamic-update-slice_fusion.refs_0_), channel_id=1, source_target_pairs={{0,8},{4,68},{8,16},{12,76},{16,24},{20,84},{24,0},{28,92},{32,40}... | collective-permute-start | bytes 2359304 | tf_op jit(solution)/shard_map/ppermute | solution.py:238
  27.7 25.6 %collective-permute-start.8 = (bf16[1024,384]{1,0:T(8,128)(2,1)}, bf16[1024,384]{1,0:T(8,128)(2,1)}, u32[]{:S(2)}, u32[]{:S(2)}) collective-permute-start(bf16[1024,384]{1,0:T(8,128)(2,1)} %constant_dynamic-update-slice_fusion.refs_0_), channel_id=1, source_target_pairs={{0,4},{4,0},{8,12},{12,8},{16,20},{20,16},{24,28},{28,24},{32,36},... | collective-permute-start | bytes 2359304 | tf_op jit(solution)/shard_map/ppermute | solution.py:238
  37.6 15.7 %collective-permute-start.10 = (bf16[1024,384]{1,0:T(8,128)(2,1)}, bf16[1024,384]{1,0:T(8,128)(2,1)}, u32[]{:S(2)}, u32[]{:S(2)}) collective-permute-start(bf16[1024,384]{1,0:T(8,128)(2,1)} %collective-permute-done.6.refs_2_), channel_id=1, source_target_pairs={{0,4},{4,0},{8,12},{12,8},{16,20},{20,16},{24,28},{28,24},{32,36},... | collective-permute-start | bytes 2359304 | tf_op jit(solution)/shard_map/ppermute | solution.py:238
  45.3 8.0 %collective-permute-start.11 = (bf16[1024,384]{1,0:T(8,128)(2,1)}, bf16[1024,384]{1,0:T(8,128)(2,1)}, u32[]{:S(2)}, u32[]{:S(2)}) collective-permute-start(bf16[1024,384]{1,0:T(8,128)(2,1)} %collective-permute-done.7.refs_3_), channel_id=1, source_target_pairs={{0,4},{4,0},{8,12},{12,8},{16,20},{20,16},{24,28},{28,24},{32,36},... | collective-permute-start | bytes 2359304 | tf_op jit(solution)/shard_map/ppermute | solution.py:238
  48.0 5.4 %collective-permute-start.9 = (bf16[1024,384]{1,0:T(8,128)(2,1)}, bf16[1024,384]{1,0:T(8,128)(2,1)}, u32[]{:S(2)}, u32[]{:S(2)}) collective-permute-start(bf16[1024,384]{1,0:T(8,128)(2,1)} %collective-permute-done.5.refs_1_), channel_id=1, source_target_pairs={{0,4},{4,0},{8,12},{12,8},{16,20},{20,16},{24,28},{28,24},{32,36},... | collective-permute-start | bytes 2359304 | tf_op jit(solution)/shard_map/ppermute | solution.py:238
  85.0 14.7 %collective-permute-start.13 = (bf16[1024,256]{1,0:T(8,128)(2,1)}, bf16[1024,256]{1,0:T(8,128)(2,1)}, u32[]{:S(2)}, u32[]{:S(2)}) collective-permute-start(bf16[1024,256]{1,0:T(8,128)(2,1)} %get-tuple-element.14), channel_id=1, source_target_pairs={{0,4},{4,0},{8,12},{12,8},{16,20},{20,16},{24,28},{28,24},{32,36},... | collective-permute-start | bytes 1572872 | tf_op jit(solution)/shard_map/ppermute | solution.py:238
  85.0 18.0 %collective-permute-start.15 = (bf16[1024,256]{1,0:T(8,128)(2,1)}, bf16[1024,256]{1,0:T(8,128)(2,1)}, u32[]{:S(2)}, u32[]{:S(2)}) collective-permute-start(bf16[1024,256]{1,0:T(8,128)(2,1)} %get-tuple-element.16), channel_id=1, source_target_pairs={{0,4},{4,0},{8,12},{12,8},{16,20},{20,16},{24,28},{28,24},{32,36},... | collective-permute-start | bytes 1572872 | tf_op jit(solution)/shard_map/ppermute | solution.py:238
  90.3 27.2 %collective-permute-start.25 = (bf16[1024,256]{1,0:T(8,128)(2,1)S(1)}, bf16[1024,256]{1,0:T(8,128)(2,1)}, u32[]{:S(2)}, u32[]{:S(2)}) collective-permute-start(bf16[1024,256]{1,0:T(8,128)(2,1)S(1)} %get-tuple-element.26), channel_id=1, source_target_pairs={{0,1},{1,2},{2,3},{3,0},{4,5},{5,6},{6,7},{7,4},{8,9},{9,10},{10,1... | collective-permute-start | bytes 1572872 | tf_op jit(solution)/shard_map/ppermute | solution.py:271
  92.4 39.4 %collective-permute-start.31 = (bf16[1024,256]{1,0:T(8,128)(2,1)S(1)}, bf16[1024,256]{1,0:T(8,128)(2,1)}, u32[]{:S(2)}, u32[]{:S(2)}) collective-permute-start(bf16[1024,256]{1,0:T(8,128)(2,1)S(1)} %get-tuple-element.25), channel_id=1, source_target_pairs={{0,3},{1,0},{2,1},{3,2},{4,7},{5,4},{6,5},{7,6},{8,11},{9,8},{10,9... | collective-permute-start | bytes 1572872 | tf_op jit(solution)/shard_map/ppermute | solution.py:271
  95.2 44.0 %collective-permute-start.28 = (bf16[1024,256]{1,0:T(8,128)(2,1)}, bf16[1024,256]{1,0:T(8,128)(2,1)}, u32[]{:S(2)}, u32[]{:S(2)}) collective-permute-start(bf16[1024,256]{1,0:T(8,128)(2,1)} %get-tuple-element.24), channel_id=1, source_target_pairs={{0,2},{1,3},{2,0},{3,1},{4,6},{5,7},{6,4},{7,5},{8,10},{9,11},{10,... | collective-permute-start | bytes 1572872 | tf_op jit(solution)/shard_map/ppermute | solution.py:271
  99.7 5.3 %collective-permute-start.17 = (bf16[1024,256]{1,0:T(8,128)(2,1)S(1)}, bf16[1024,256]{1,0:T(8,128)(2,1)S(1)}, u32[]{:S(2)}, u32[]{:S(2)}) collective-permute-start(bf16[1024,256]{1,0:T(8,128)(2,1)S(1)} %copy-done.11), channel_id=1, source_target_pairs={{0,4},{4,0},{8,12},{12,8},{16,20},{20,16},{24,28},{28,24},{32,36},... | collective-permute-start | bytes 1572872 | tf_op jit(solution)/shard_map/ppermute | solution.py:238
  103.0 42.7 %collective-permute-start.12 = (bf16[1024,256]{1,0:T(8,128)(2,1)}, bf16[1024,256]{1,0:T(8,128)(2,1)}, u32[]{:S(2)}, u32[]{:S(2)}) collective-permute-start(bf16[1024,256]{1,0:T(8,128)(2,1)} %get-tuple-element.12), channel_id=1, source_target_pairs={{0,4},{4,0},{8,12},{12,8},{16,20},{20,16},{24,28},{28,24},{32,36},... | collective-permute-start | bytes 1572872 | tf_op jit(solution)/shard_map/ppermute | solution.py:238
  105.0 40.8 %collective-permute-start.14 = (bf16[1024,256]{1,0:T(8,128)(2,1)}, bf16[1024,256]{1,0:T(8,128)(2,1)}, u32[]{:S(2)}, u32[]{:S(2)}) collective-permute-start(bf16[1024,256]{1,0:T(8,128)(2,1)} %add_convert_fusion.3), channel_id=1, source_target_pairs={{0,24},{4,196},{8,0},{12,204},{16,8},{20,212},{24,16},{28,220},{32... | collective-permute-start | bytes 1572872 | tf_op jit(solution)/shard_map/ppermute | solution.py:238
  117.5 28.7 %collective-permute-start.16 = (bf16[1024,256]{1,0:T(8,128)(2,1)}, bf16[1024,256]{1,0:T(8,128)(2,1)S(1)}, u32[]{:S(2)}, u32[]{:S(2)}) collective-permute-start(bf16[1024,256]{1,0:T(8,128)(2,1)} %add_convert_fusion.2), channel_id=1, source_target_pairs={{0,16},{4,132},{8,24},{12,140},{16,0},{20,148},{24,8},{28,156},{32... | collective-permute-start | bytes 1572872 | tf_op jit(solution)/shard_map/ppermute | solution.py:238
  131.7 18.5 %collective-permute-start.18 = (bf16[1024,256]{1,0:T(8,128)(2,1)}, bf16[1024,256]{1,0:T(8,128)(2,1)}, u32[]{:S(2)}, u32[]{:S(2)}) collective-permute-start(bf16[1024,256]{1,0:T(8,128)(2,1)} %add_convert_fusion.1), channel_id=1, source_target_pairs={{0,8},{4,68},{8,16},{12,76},{16,24},{20,84},{24,0},{28,92},{32,40}... | collective-permute-start | bytes 1572872 | tf_op jit(solution)/shard_map/ppermute | solution.py:238
  139.2 16.0 %collective-permute-start.26 = (bf16[1024,256]{1,0:T(8,128)(2,1)}, bf16[1024,256]{1,0:T(8,128)(2,1)S(1)}, u32[]{:S(2)}, u32[]{:S(2)}) collective-permute-start(bf16[1024,256]{1,0:T(8,128)(2,1)} %collective-permute-done.25), channel_id=1, source_target_pairs={{0,4},{4,0},{8,12},{12,8},{16,20},{20,16},{24,28},{28,24},{32,36},... | collective-permute-start | bytes 1572872 | tf_op jit(solution)/shard_map/ppermute | solution.py:238
  145.7 21.1 %collective-permute-start.32 = (bf16[1024,256]{1,0:T(8,128)(2,1)}, bf16[1024,256]{1,0:T(8,128)(2,1)S(1)}, u32[]{:S(2)}, u32[]{:S(2)}) collective-permute-start(bf16[1024,256]{1,0:T(8,128)(2,1)} %collective-permute-done.31), channel_id=1, source_target_pairs={{0,4},{4,0},{8,12},{12,8},{16,20},{20,16},{24,28},{28,24},{32,36},... | collective-permute-start | bytes 1572872 | tf_op jit(solution)/shard_map/ppermute | solution.py:238
  145.8 27.3 %collective-permute-start.29 = (bf16[1024,256]{1,0:T(8,128)(2,1)}, bf16[1024,256]{1,0:T(8,128)(2,1)S(1)}, u32[]{:S(2)}, u32[]{:S(2)}) collective-permute-start(bf16[1024,256]{1,0:T(8,128)(2,1)} %collective-permute-done.28), channel_id=1, source_target_pairs={{0,4},{4,0},{8,12},{12,8},{16,20},{20,16},{24,28},{28,24},{32,36},... | collective-permute-start | bytes 1572872 | tf_op jit(solution)/shard_map/ppermute | solution.py:238
  152.0 4.7 %collective-permute-start.19 = (bf16[256,256]{1,0:T(8,128)(2,1)S(1)}, bf16[256,256]{1,0:T(8,128)(2,1)S(1)}, u32[]{:S(2)}, u32[]{:S(2)}) collective-permute-start(bf16[256,256]{1,0:T(8,128)(2,1)S(1)} %get-tuple-element.27), channel_id=1, source_target_pairs={{0,192},{4,28},{8,200},{12,4},{16,208},{20,12},{24,216},{28,20},{3... | collective-permute-start | bytes 393224 | tf_op jit(solution)/shard_map/ppermute | solution.py:238
  152.1 5.6 %collective-permute-start.20 = (bf16[256,256]{1,0:T(8,128)(2,1)S(1)}, bf16[256,256]{1,0:T(8,128)(2,1)S(1)}, u32[]{:S(2)}, u32[]{:S(2)}) collective-permute-start(bf16[256,256]{1,0:T(8,128)(2,1)S(1)} %get-tuple-element.29), channel_id=1, source_target_pairs={{0,128},{4,20},{8,136},{12,28},{16,144},{20,4},{24,152},{28,12},{3... | collective-permute-start | bytes 393224 | tf_op jit(solution)/shard_map/ppermute | solution.py:238
  155.3 5.0 %collective-permute-start.21 = (bf16[256,256]{1,0:T(8,128)(2,1)S(1)}, bf16[256,256]{1,0:T(8,128)(2,1)S(1)}, u32[]{:S(2)}, u32[]{:S(2)}) collective-permute-start(bf16[256,256]{1,0:T(8,128)(2,1)S(1)} %get-tuple-element.28), channel_id=1, source_target_pairs={{0,64},{4,12},{8,72},{12,20},{16,80},{20,28},{24,88},{28,4},{32,96... | collective-permute-start | bytes 393224 | tf_op jit(solution)/shard_map/ppermute | solution.py:238
  160.4 8.9 %collective-permute-start.22 = (bf16[128,256]{1,0:T(8,128)(2,1)S(1)}, bf16[128,256]{1,0:T(8,128)(2,1)S(1)}, u32[]{:S(2)}, u32[]{:S(2)}) collective-permute-start(bf16[128,256]{1,0:T(8,128)(2,1)S(1)} %slice.77), channel_id=1, source_target_pairs={{0,32},{4,36},{8,40},{12,44},{16,48},{20,52},{24,56},{28,60},{32,0... | collective-permute-start | bytes 196616 | tf_op jit(solution)/shard_map/ppermute | solution.py:238
  169.9 8.5 %collective-permute-start.23 = (bf16[64,256]{1,0:T(8,128)(2,1)}, bf16[64,256]{1,0:T(8,128)(2,1)}, u32[]{:S(2)}, u32[]{:S(2)}) collective-permute-start(bf16[64,256]{1,0:T(8,128)(2,1)} %slice.97), channel_id=1, source_target_pairs={{0,4},{4,0},{8,12},{12,8},{16,20},{20,16},{24,28},{28,24},{32,36},... | collective-permute-start | bytes 98312 | tf_op jit(solution)/shard_map/ppermute | solution.py:238
  179.7 11.7 %collective-permute-start.24 = (bf16[128,256]{1,0:T(8,128)(2,1)S(1)}, bf16[128,256]{1,0:T(8,128)(2,1)S(1)}, u32[]{:S(2)}, u32[]{:S(2)}) collective-permute-start(bf16[128,256]{1,0:T(8,128)(2,1)S(1)} %pad_maximum_fusion.6), channel_id=1, source_target_pairs={{0,1},{1,2},{2,3},{3,0},{4,5},{5,6},{6,7},{7,4},{8,9},{9,10},{10,1... | collective-permute-start | bytes 196616 | tf_op jit(solution)/shard_map/ppermute | solution.py:341
  185.9 7.4 %collective-permute-start.30 = (bf16[128,256]{1,0:T(8,128)(2,1)S(1)}, bf16[128,256]{1,0:T(8,128)(2,1)S(1)}, u32[]{:S(2)}, u32[]{:S(2)}) collective-permute-start(bf16[128,256]{1,0:T(8,128)(2,1)S(1)} %pad_maximum_fusion.6), channel_id=1, source_target_pairs={{0,3},{1,0},{2,1},{3,2},{4,7},{5,4},{6,5},{7,6},{8,11},{9,8},{10,9... | collective-permute-start | bytes 196616 | tf_op jit(solution)/shard_map/ppermute | solution.py:341
  185.9 7.9 %collective-permute-start.27 = (bf16[128,256]{1,0:T(8,128)(2,1)S(1)}, bf16[128,256]{1,0:T(8,128)(2,1)S(1)}, u32[]{:S(2)}, u32[]{:S(2)}) collective-permute-start(bf16[128,256]{1,0:T(8,128)(2,1)S(1)} %pad_maximum_fusion.6), channel_id=1, source_target_pairs={{0,2},{1,3},{2,0},{3,1},{4,6},{5,7},{6,4},{7,5},{8,10},{9,11},{10,... | collective-permute-start | bytes 196616 | tf_op jit(solution)/shard_map/ppermute | solution.py:341
  (22 other events, 302.0 us)

commit v2 on v0

v2 whole, which is shorter than its diff:
```python
import functools
import math

import jax
import jax.numpy as jnp
from jax import lax
from jax.experimental import pallas as pl
from jax.experimental.pallas import tpu as pltpu
from jax.sharding import Mesh
from jax.sharding import PartitionSpec as P

rope_base = 500000.0
big_negative = -1e30
n_ctx = 64
n_head = 4
block_len = 64
key_span = 256
granule = 16
log2e = 1.4426950408889634


swap = [(0, 1), (1, 0)]
both_swap = [(0, 3), (1, 2), (2, 1), (3, 0)]


def head_perm(s):
    return [(h, (h + s) % n_head) for h in range(n_head)]


def rotation_tables(positions, width):
    half_width = width // 2
    exponent = jnp.arange(half_width, dtype=jnp.float32) * (2.0 / width)
    frequency = jnp.exp(-math.log(rope_base) * exponent)
    angles = positions.astype(jnp.float32)[:, None] * frequency[None, :]
    return (jnp.cos(angles), jnp.sin(angles))


def rotate(vectors, cos_table, sin_table):
    half_width = vectors.shape[1] // 2
    a = vectors[:, :half_width]
    b = vectors[:, half_width:]
    return jnp.concatenate([a * cos_table - b * sin_table, b * cos_table + a * sin_table], axis=1)


def unrotate(vectors, cos_table, sin_table):
    return rotate(vectors, cos_table, -sin_table)


def granule_rows(index):
    return pl.ds(pl.multiple_of(index * granule, granule), granule)


def load_operands(order_ref, gathered, packs, kv, q_rows, g_rows, starts):
    tokens = kv.shape[0] - key_span
    kv[tokens:, :] = jnp.zeros_like(kv[tokens:, :])

    def fetch(i, carry):
        kv[granule_rows(order_ref[i]), :] = gathered[granule_rows(i), :]
        return carry

    lax.fori_loop(0, tokens // granule, fetch, 0, unroll=8)
    head_dim = q_rows.shape[1]
    half = starts.shape[1]
    for rel in range(4):
        pack = packs[rel]
        code = pack[256:272, :].astype(jnp.float32)
        start = (code[0:1, :] * 128.0 + code[1:2, :]).astype(jnp.int32)
        for block in range(2):
            part = rel * 2 + block
            starts[part : part + 1, :] = start[:, block * half : (block + 1) * half]
            for group in range(half // block_len):
                to = pl.ds(part * half + group * block_len, block_len)
                cols = pl.ds(group * head_dim, head_dim)
                q_rows[to, :] = pack[block * block_len : (block + 1) * block_len, cols]
                g_rows[to, :] = pack[128 + block * block_len : 128 + (block + 1) * block_len, cols]


def query_part(place_ref, part, half):
    block = place_ref[1 + part]
    first_block = place_ref[9 + part] // block_len
    tiles = ((block - first_block + 1) * granule + key_span - 1) // key_span
    lane = lax.broadcasted_iota(jnp.int32, (1, half), 1)
    return first_block, tiles, place_ref[17 + part], block * block_len + lane % block_len


chunk = 512
contract_last = (((1,), (1,)), ((), ()))


def tile_rows(kt, first_block, place_ref):
    base = first_block * granule + kt * key_span
    offset = (first_block + kt * (key_span // granule)) * block_len + place_ref[0] * granule
    return pl.ds(pl.multiple_of(base, granule), key_span), offset


def fill_positions(key_rel):
    row = lax.broadcasted_iota(jnp.int32, key_rel.shape, 0)
    key_rel[...] = (row // granule) * block_len + row % granule


def chunk_terms(key, value, q_wide, g_part, pos, start, key_rel, factor):
    score = lax.dot_general(key, q_wide, contract_last, preferred_element_type=jnp.float32) * factor
    prob_grad = lax.dot_general(value, g_part, contract_last, preferred_element_type=jnp.float32)
    live = (key_rel <= pos) & (key_rel >= start)
    return score, prob_grad, live


def stats_kernel(place_ref, order_ref, *refs, factor):
    gathered, packs, stats_ref = refs[0], refs[1:5], refs[5]
    kv, q_rows, g_rows, starts, key_rel = refs[6:]
    load_operands(order_ref, gathered, packs, kv, q_rows, g_rows, starts)
    half = starts.shape[1]
    head_dim = q_rows.shape[1]
    fill_positions(key_rel)

    def one_part(part, carry):
        first_block, tiles, slot, pos = query_part(place_ref, part, half)
        cols = pl.ds(pl.multiple_of(part * half, half), half)
        start = starts[pl.ds(part, 1), :]

        def stats(kt, carried):
            rows, offset = tile_rows(kt, first_block, place_ref)
            key = kv[rows, : 2 * head_dim]
            value = kv[rows, 2 * head_dim :]
            result = []
            for c in range(half // chunk):
                top, total, weighted = carried[c]
                at = slice(c * chunk, (c + 1) * chunk)
                to = pl.ds(pl.multiple_of(part * half + c * chunk, chunk), chunk)
                q_part = q_rows[to, :]
                score, prob_grad, live = chunk_terms(
                    key,
                    value,
                    jnp.concatenate([q_part, q_part], axis=1),
                    g_rows[to, :],
                    pos[:, at] - offset,
                    start[:, at] - offset,
                    key_rel[...],
                    factor,
                )
                score = jnp.where(live, score, big_negative)
                new_top = jnp.maximum(top, jnp.max(score, axis=0, keepdims=True))
                growth = jnp.exp2(score - new_top)
                faded = jnp.exp2(top - new_top)
                result.append(
                    (
                        new_top,
                        total * faded + jnp.sum(growth, axis=0, keepdims=True),
                        weighted * faded + jnp.sum(growth * prob_grad, axis=0, keepdims=True),
                    )
                )
            return tuple(result)

        row = (1, chunk)
        zero = jnp.zeros(row, jnp.float32)
        init = (jnp.full(row, big_negative, jnp.float32), zero, zero)
        carried = lax.fori_loop(0, tiles, stats, (init,) * (half // chunk))
        top, total, weighted = (jnp.concatenate(v, axis=1) for v in zip(*carried))
        stats_ref[pl.ds(slot, 1), :] = top + jnp.log2(total)
        stats_ref[pl.ds(8 + slot, 1), :] = weighted / total
        return carry

    lax.fori_loop(0, 8, one_part, 0)


def grads_kernel(place_ref, order_ref, *refs, factor, scaling):
    gathered, packs, stats = refs[0], refs[1:5], refs[5:9]
    out_ref, dq_ref = refs[9:11]
    kv, q_rows, g_rows, starts, key_rel, acc, dq_acc, logs, deltas = refs[11:]
    load_operands(order_ref, gathered, packs, kv, q_rows, g_rows, starts)
    half = starts.shape[1]
    head_dim = q_rows.shape[1]
    acc[...] = jnp.zeros_like(acc)
    fill_positions(key_rel)

    top = jnp.maximum(
        jnp.maximum(stats[0][:8, :], stats[1][:8, :]), jnp.maximum(stats[2][:8, :], stats[3][:8, :])
    )
    total = jnp.zeros_like(top)
    weighted = jnp.zeros_like(top)
    for s in stats:
        share = jnp.exp2(s[:8, :] - top)
        total = total + share
        weighted = weighted + share * s[8:, :]
    logs[...] = top + jnp.log2(total)
    deltas[...] = weighted / total

    def one_part(part, carry):
        first_block, tiles, slot, pos = query_part(place_ref, part, half)
        cols = pl.ds(pl.multiple_of(part * half, half), half)
        start = starts[pl.ds(part, 1), :]
        log_total = logs[pl.ds(slot, 1), :]
        delta = deltas[pl.ds(slot, 1), :]
        dq_acc[...] = jnp.zeros_like(dq_acc)

        def grads(kt, carry):
            rows, offset = tile_rows(kt, first_block, place_ref)
            key = kv[rows, : 2 * head_dim]
            value = kv[rows, 2 * head_dim :]
            key_t = key.T
            key_sum = acc[rows, :head_dim]
            value_sum = acc[rows, head_dim:]
            for c in range(half // chunk):
                at = slice(c * chunk, (c + 1) * chunk)
                to = pl.ds(pl.multiple_of(part * half + c * chunk, chunk), chunk)
                q_part = q_rows[to, :]
                g_part = g_rows[to, :]
                score, prob_grad, live = chunk_terms(
                    key,
                    value,
                    jnp.concatenate([q_part, q_part], axis=1),
                    g_part,
                    pos[:, at] - offset,
                    start[:, at] - offset,
                    key_rel[...],
                    factor,
                )
                prob = jnp.where(live, jnp.exp2(score - log_total[:, at]), 0.0)
                score_grad = (prob * ((prob_grad - delta[:, at]) * scaling)).astype(jnp.bfloat16)
                key_sum += jnp.dot(score_grad, q_part, preferred_element_type=jnp.float32)
                value_sum += jnp.dot(
                    prob.astype(jnp.bfloat16), g_part, preferred_element_type=jnp.float32
                )
                dq_acc[:, at] += jnp.dot(key_t, score_grad, preferred_element_type=jnp.float32)
            acc[rows, :head_dim] = key_sum
            acc[rows, head_dim:] = value_sum
            return carry

        lax.fori_loop(0, tiles, grads, 0)
        dq = (dq_acc[:head_dim, :] + dq_acc[head_dim:, :]).T
        to = pl.ds(pl.multiple_of(part * block_len, block_len), block_len)
        for group in range(half // block_len):
            dq_ref[to, group * head_dim : (group + 1) * head_dim] = dq[
                group * block_len : (group + 1) * block_len, :
            ]
        return carry

    lax.fori_loop(0, 8, one_part, 0)

    def store(i, carry):
        out_ref[granule_rows(i), :] = acc[granule_rows(order_ref[i]), :].astype(jnp.bfloat16)
        return carry

    lax.fori_loop(0, out_ref.shape[0] // granule, store, 0, unroll=8)


def kernel_scratch(quarter, head_dim, rows):
    half = rows // 2
    return [
        pltpu.VMEM((quarter + key_span, 3 * head_dim), jnp.bfloat16),
        pltpu.VMEM((4 * rows, head_dim), jnp.bfloat16),
        pltpu.VMEM((4 * rows, head_dim), jnp.bfloat16),
        pltpu.VMEM((8, half), jnp.int32),
        pltpu.VMEM((key_span, chunk), jnp.int32),
    ]


def run_stats(place, order, gathered, packs, scaling, tokens, head_dim, rows):
    smem = pl.BlockSpec(memory_space=pltpu.SMEM)
    vmem = pl.BlockSpec(memory_space=pltpu.VMEM)
    return pl.pallas_call(
        functools.partial(stats_kernel, factor=scaling * log2e),
        out_shape=jax.ShapeDtypeStruct((16, rows // 2), jnp.float32),
        in_specs=[smem, smem] + [vmem] * 5,
        out_specs=vmem,
        scratch_shapes=kernel_scratch(tokens // 4, head_dim, rows),
        compiler_params=pltpu.CompilerParams(vmem_limit_bytes=32 * 1024 * 1024),
        cost_estimate=pl.CostEstimate(
            flops=8 * rows * tokens * head_dim,
            bytes_accessed=4 * 1024 * 1024,
            transcendentals=rows * tokens // 2,
        ),
    )(place, order, gathered, *packs)


def run_grads(place, order, gathered, packs, stats, scaling, tokens, head_dim, rows):
    smem = pl.BlockSpec(memory_space=pltpu.SMEM)
    vmem = pl.BlockSpec(memory_space=pltpu.VMEM)
    quarter = tokens // 4
    half = rows // 2
    return pl.pallas_call(
        functools.partial(grads_kernel, factor=scaling * log2e, scaling=scaling),
        out_shape=[
            jax.ShapeDtypeStruct((quarter, 2 * head_dim), jnp.bfloat16),
            jax.ShapeDtypeStruct((8 * block_len, (half // block_len) * head_dim), jnp.float32),
        ],
        in_specs=[smem, smem] + [vmem] * 9,
        out_specs=[vmem] * 2,
        scratch_shapes=kernel_scratch(quarter, head_dim, rows)
        + [
            pltpu.VMEM((quarter + key_span, 2 * head_dim), jnp.float32),
            pltpu.VMEM((2 * head_dim, half), jnp.float32),
            pltpu.VMEM((8, half), jnp.float32),
            pltpu.VMEM((8, half), jnp.float32),
        ],
        compiler_params=pltpu.CompilerParams(vmem_limit_bytes=40 * 1024 * 1024),
        cost_estimate=pl.CostEstimate(
            flops=16 * rows * tokens * head_dim,
            bytes_accessed=8 * 1024 * 1024,
            transcendentals=rows * tokens // 2,
        ),
    )(place, order, gathered, *packs, *stats)


def product_kernel(place_ref, back_ref, key_ref, value_ref, *refs):
    near, far, near_core, far_core, out_ref = refs
    head = place_ref[0]
    contract = (((1,), (1,)), ((), ()))
    width = 2 * key_ref.shape[1]
    span = near.shape[1]

    def share(source):
        return back_ref[:, pl.ds(pl.multiple_of(source * width, width), width)]

    def times(left, right):
        return lax.dot_general(left, right, contract, preferred_element_type=jnp.float32)

    backs = [share((head + n_head - s) % n_head) for s in range(n_head)]
    for rel, piece in enumerate((near, near_core, far, far_core)):
        at = pl.ds(pl.multiple_of(place_ref[1 + rel] * span, span), span)
        own = jnp.concatenate([key_ref[at, :], value_ref[at, :]], axis=1)
        total = times(backs[0], own)
        for s in range(1, n_head):
            total += times(backs[s], piece[s - 1])
        out_ref[:, at] = total.astype(jnp.bfloat16)


def run_product(place, back, key_own, value_own, pieces):
    smem = pl.BlockSpec(memory_space=pltpu.SMEM)
    vmem = pl.BlockSpec(memory_space=pltpu.VMEM)
    out_width = key_own.shape[0]
    return pl.pallas_call(
        product_kernel,
        out_shape=jax.ShapeDtypeStruct((back.shape[0], out_width), jnp.bfloat16),
        in_specs=[smem] + [vmem] * 7,
        out_specs=vmem,
        compiler_params=pltpu.CompilerParams(vmem_limit_bytes=24 * 1024 * 1024),
        cost_estimate=pl.CostEstimate(
            flops=2 * back.shape[0] * back.shape[1] * out_width,
            bytes_accessed=5 * 1024 * 1024,
            transcendentals=0,
        ),
    )(place, back, key_own, value_own, *pieces)


def flip(v, axis, when):
    return jnp.where(when, jnp.flip(v, axis), v)


def shards(layer_input, key_weight, value_weight, queries, out_grad, doc_start, block_order):
    f32, bf16 = jnp.float32, jnp.bfloat16
    row_count = layer_input.shape[0]
    tokens = row_count * n_ctx
    head_dim = key_weight.shape[1]
    width = key_weight.shape[0]
    groups = queries.shape[1] // head_dim
    rows = row_count * groups
    scaling = 1.0 / math.sqrt(head_dim)
    x, y = lax.axis_index("x"), lax.axis_index("y")
    z, core, head = lax.axis_index("zl"), lax.axis_index("core"), lax.axis_index("head")
    z_is_one, core_is_one = z == 1, core == 1

    def pick(v, index, axis):
        return lax.dynamic_index_in_dim(v, index, axis, keepdims=False)

    order = block_order.reshape(4, 2, 4, 2, 2).transpose(0, 2, 1, 3, 4)
    order = flip(flip(order, 2, z_is_one), 3, core_is_one)
    node_blocks = pick(pick(order, x, 0), y, 0).reshape(8)

    own_blocks = node_blocks[:2]
    own_pos = (
        own_blocks[:, None] * block_len + jnp.arange(block_len, dtype=jnp.int32)[None, :]
    ).reshape(-1)
    cos_own, sin_own = rotation_tables(own_pos, head_dim)
    key_raw = jnp.dot(layer_input, key_weight, preferred_element_type=f32)
    keys = rotate(key_raw, cos_own, sin_own)
    key_hi = lax.reduce_precision(keys, 8, 7)
    key_lo = keys - key_hi
    values = jnp.dot(layer_input, value_weight, preferred_element_type=f32)
    local = jnp.concatenate(
        [key_hi.astype(bf16), key_lo.astype(bf16), values.astype(bf16)], axis=1
    ).reshape(2, 2, 2, granule, 3 * head_dim)

    pair = jnp.stack(
        [pick(local, core, 2), lax.ppermute(pick(local, 1 - core, 2), "core", swap)]
    )
    node = jnp.stack([pick(pair, z, 2), lax.ppermute(pick(pair, 1 - z, 2), "zl", swap)])
    node = node.reshape(1, row_count, 3 * head_dim)

    def per_column(v):
        return jnp.broadcast_to(v.reshape(2, 1, block_len), (2, groups, block_len)).reshape(1, rows)

    start_cols = per_column(doc_start)
    start_code = jnp.concatenate(
        [start_cols // 128, start_cols % 128, jnp.zeros((14, rows), jnp.int32)], axis=0
    ).astype(bf16)
    pack_own = jnp.concatenate([queries, out_grad, start_code], axis=0)
    node, pack_sent = lax.optimization_barrier((node, pack_own))
    pack_z = lax.ppermute(pack_sent, "zl", swap)
    packs = [
        pack_own,
        lax.ppermute(pack_own, "core", swap),
        pack_z,
        lax.ppermute(pack_z, "core", swap),
    ]

    out_width = width // n_head
    span = out_width // 4
    quarter = z * 2 + core

    def weight_part(to_head):
        at = to_head * out_width + quarter * span
        return jnp.concatenate(
            [lax.dynamic_slice_in_dim(w, at, span) for w in (key_weight, value_weight)], axis=1
        )

    weight_parts = [weight_part((head + s) % n_head) for s in (1, 2, 3)]
    key_own = lax.dynamic_slice_in_dim(key_weight, head * out_width, out_width)
    value_own = lax.dynamic_slice_in_dim(value_weight, head * out_width, out_width)
    node, weight_parts = lax.optimization_barrier((node, weight_parts))
    weights_near = [
        lax.ppermute(w, "head", head_perm(s)) for w, s in zip(weight_parts, (1, 2, 3))
    ]

    gathered = lax.all_to_all(
        jnp.broadcast_to(node, (16, row_count, 3 * head_dim)), ("x", "y"), 0, 0
    ).reshape(tokens // 4, 3 * head_dim)

    codes = jnp.stack([p[256:258, :: rows // 2] for p in packs]).astype(f32)
    firsts = (codes[:, 0] * 128.0 + codes[:, 1]).astype(jnp.int32).reshape(8)
    slots = jnp.arange(8, dtype=jnp.int32).reshape(2, 2, 2)
    slots = flip(flip(slots, 0, z_is_one), 1, core_is_one).reshape(8)
    place = jnp.concatenate([quarter[None], node_blocks, firsts, slots]).astype(jnp.int32)
    table = order.reshape(tokens // block_len)
    stats = run_stats(place, table, gathered, packs, scaling, tokens, head_dim, rows)
    stats_all = [
        stats,
        lax.ppermute(stats, "core", swap),
        lax.ppermute(stats, "zl", swap),
        lax.ppermute(stats, ("zl", "core"), both_swap),
    ]
    stats_all, weights_near = lax.optimization_barrier((stats_all, weights_near))
    weights_near = jnp.stack(weights_near)
    weights_far = lax.ppermute(weights_near, "zl", swap)
    grads, dq = run_grads(
        place, table, gathered, packs, stats_all, scaling, tokens, head_dim, rows
    )
    grads, weights_far = lax.optimization_barrier((grads, weights_far))
    weights = [
        weights_near,
        weights_far,
        lax.ppermute(weights_near, "core", swap),
        lax.ppermute(weights_far, "core", swap),
    ]

    grads = lax.all_to_all(
        grads.reshape(16, row_count, 2 * head_dim), ("x", "y"), 0, 0
    )
    grads = jnp.sum(grads.astype(f32), axis=0)
    quarter_pos = (
        node_blocks[:, None] * block_len
        + quarter * granule
        + jnp.arange(granule, dtype=jnp.int32)[None, :]
    ).reshape(-1)
    cos_node, sin_node = rotation_tables(quarter_pos, head_dim)
    key_back = unrotate(grads[:, :head_dim], cos_node, sin_node).astype(bf16)
    back = jnp.concatenate([key_back, grads[:, head_dim:].astype(bf16)], axis=1)

    back = back.reshape(2, 2, 2, granule, 2 * head_dim)
    back = jnp.stack([back[:, 0], lax.ppermute(back[:, 1], "core", swap)], axis=1)
    back = flip(flip(back, 0, z_is_one), 1, core_is_one)
    back = jnp.broadcast_to(back[:, None], (2, n_head) + back.shape[1:]).reshape(
        8, row_count // 2, 2 * head_dim
    )
    back = lax.all_to_all(back, ("zl", "head"), 0, 0)
    back = back.reshape(2, n_head, 2, 2, granule, 2 * head_dim)
    back = back.transpose(3, 0, 2, 4, 1, 5).reshape(row_count, n_head * 2 * head_dim)

    product_place = jnp.stack([head, quarter, quarter ^ 1, quarter ^ 2, quarter ^ 3])
    input_grad = run_product(product_place.astype(jnp.int32), back, key_own, value_own, weights)

    dq = dq.reshape(2, 2 * row_count, groups * head_dim)
    dq = dq[0] + lax.ppermute(dq[1].astype(bf16), "zl", swap).astype(f32)
    query_grad = dq[:row_count] + lax.ppermute(dq[row_count:], "core", swap)
    return (input_grad, query_grad.astype(bf16))


def solution(mesh):
    ctx = ("x", "zl", "y", "core")
    split = Mesh(mesh.devices.reshape(4, 2, 4, 2, n_head), ctx + ("head",))
    return jax.shard_map(
        shards,
        mesh=split,
        in_specs=(
            P(ctx, None),
            P(None, "head"),
            P(None, "head"),
            P(ctx, "head"),
            P(ctx, "head"),
            P(ctx),
            P(),
        ),
        out_specs=(P(ctx, "head"), P(ctx, "head")),
        check_vma=False,
    )
```

time: 1150 us -> 147 us (0.13)
  the two profiles are of different devices: /device:TPU:1 before, /device:TPU:32 now
where the time goes in v2:
time: 147 us; the launch traced here: 146 us
  waiting for transfers between devices  45 us (31%)
  starting transfers between devices  36.9 us (25%)
  Pallas kernels  27.1 us (18%)
  local copies, waits for them, and re-layouts  22 us (15%)
  other arithmetic  10.5 us (7%)
  matrix products  3.64 us (2%)
    all_to_all x1, waiting for transfers between devices, shards(): lax.all_to_all(grads.reshape(16, row_count, 2 * head_dim), ('x', 'y'), 0, 0)  14.5 us
    pallas_call x1, Pallas kernels, run_grads(): pl.pallas_call(functools.partial(grads_kernel, factor=scaling * log2e, sc...  14.2 us
    ppermute x1, waiting for transfers between devices, shards(): pack_z = lax.ppermute(pack_sent, 'zl', swap)  13.1 us
    ppermute x3, waiting for transfers between devices, shards(): lax.ppermute(w, 'head', head_perm(s))  9.42 us
    ppermute x3, starting transfers between devices, shards(): lax.ppermute(w, 'head', head_perm(s))  9.29 us
    pallas_call x1, Pallas kernels, run_stats(): pl.pallas_call(functools.partial(stats_kernel, factor=scaling * log2e), o...  8.98 us
    all_to_all x1, starting transfers between devices, shards(): lax.all_to_all(grads.reshape(16, row_count, 2 * head_dim), ('x', 'y'), 0, 0)  8.42 us
    all_to_all x1, waiting for transfers between devices, shards(): back = lax.all_to_all(back, ('zl', 'head'), 0, 0)  7.22 us
  transfers between devices with their start and end apart: 20, of which 8 were waited for; matrix products, arithmetic and copies ran while one was open for 15% of the time, Pallas kernels for 16%

profile of v2, /device:TPU:32, one launch (start us, length us, event | category | flops | bytes accessed | tf_op | source)
XLA Modules:
  0.0 146.3 jit_solution(16062926471959128671)
XLA Ops:
  2.2 2.7 %fusion.26 = f32[128,128]{0,1:T(8,128)S(1)} fusion(bf16[128,8192]{1,0:T(8,128)(2,1)S(1)} %copy-done, bf16[8192,128]{1,0:T(8,128)(2,1)} %param.8), kind=kOutput, calls=%fused_computation.86 | convolution fusion | flops 268435456 | bytes 4259840 | tf_op jit(solution)/shard_map/dot_general | solution.py:375
  6.7 1.3 constant_dynamic-slice_fusion.2
  9.5 1.9 %collective-permute-start.2 = (bf16[2,2,16,384]{3,2,1,0:T(8,128)(2,1)S(1)}, bf16[2,2,16,384]{3,2,1,0:T(8,128)(2,1)S(1)}, u32[]{:S(2)}, u32[]{:S(2)}) collective-permute-start(bf16[2,2,16,384]{3,2,1,0:T(8,128)(2,1)S(1)} %get-tuple-element.47), channel_id=1, source_target_pairs={{0,32},{32,0},{1,33},{33,1},{2,34},{34,2},{3,35},{35,3},{4,36},{36... | collective-permute-start | bytes 147464 | tf_op jit(solution)/shard_map/ppermute | solution.py:387
  12.2 1.3 concatenate.33.refs_1_
  13.8 1.4 broadcast_in_dim.16
  15.2 7.0 %all-to-all-start = ((bf16[16,128,384]{2,1,0:T(8,128)(2,1)}), bf16[16,128,384]{2,1,0:T(8,128)(2,1)}, u32[]{:S(2)}, u32[]{:S(2)}) async-start(bf16[16,128,384]{2,1,0:T(8,128)(2,1)} %broadcast_in_dim.16), calls=%async_computation | async-start | bytes 3145728 | tf_op jit(solution)/shard_map/all_to_all | solution.py:425
  22.7 13.1 %collective-permute-done.3.refs_3_ = bf16[272,1024]{1,0:T(8,128)(2,1)S(1)} collective-permute-done((bf16[272,1024]{1,0:T(8,128)(2,1)S(1)}, bf16[272,1024]{1,0:T(8,128)(2,1)S(1)}, u32[]{:S(2)}, u32[]{:S(2)}) %collective-permute-start.3) | collective-permute-done | bytes 557088 | tf_op jit(solution)/shard_map/ppermute | solution.py:399
  36.1 5.5 %collective-permute-start.10 = (bf16[512,256]{1,0:T(8,128)(2,1)}, bf16[512,256]{1,0:T(8,128)(2,1)}, u32[]{:S(2)}, u32[]{:S(2)}) collective-permute-start(bf16[512,256]{1,0:T(8,128)(2,1)} %pad_maximum_fusion.3), channel_id=1, source_target_pairs={{0,3},{1,0},{2,1},{3,2},{4,7},{5,4},{6,5},{7,6},{8,11},{9,8},{10,9... | collective-permute-start | bytes 786440 | tf_op jit(solution)/shard_map/ppermute | solution.py:422
  41.6 3.8 %collective-permute-start.9 = (bf16[512,256]{1,0:T(8,128)(2,1)}, bf16[512,256]{1,0:T(8,128)(2,1)}, u32[]{:S(2)}, u32[]{:S(2)}) collective-permute-start(bf16[512,256]{1,0:T(8,128)(2,1)} %pad_maximum_fusion.2), channel_id=1, source_target_pairs={{0,2},{1,3},{2,0},{3,1},{4,6},{5,7},{6,4},{7,5},{8,10},{9,11},{10,... | collective-permute-start | bytes 786440 | tf_op jit(solution)/shard_map/ppermute | solution.py:422
  47.3 9.0 %shard_map.86.refs_5_ = f32[16,512]{1,0:T(8,128)S(1)} custom-call(s32[25]{0:T(128)S(1)} %pad_add_fusion.place_ref, s32[128]{0:T(128)S(1)} %reshape.283.order_ref, bf16[2048,384]{1,0:T(8,128)(2,1)} %bitcast.19.refs_0_, bf16[272,1024]{1,0:T(8,128)(2,1)S(1)} %concatenate.33.refs_1_, bf16[272,1024]{1,0:T(8,128)(2,1)} %collective-permute-done.refs_2_, ...), custom_call_target="tpu_custom_call" | custom-call | flops 8589934592 | bytes 4194304 | tf_op jit(solution)/shard_map/pallas_call | solution.py:261
  56.4 1.1 collective-permute-start.6
  58.3 6.1 %collective-permute-done.8 = bf16[512,256]{1,0:T(8,128)(2,1)} collective-permute-done((bf16[512,256]{1,0:T(8,128)(2,1)}, bf16[512,256]{1,0:T(8,128)(2,1)}, u32[]{:S(2)}, u32[]{:S(2)}) %collective-permute-start.8) | collective-permute-done | bytes 262176 | tf_op jit(solution)/shard_map/ppermute | solution.py:422
  64.3 3.0 %collective-permute-done.9 = bf16[512,256]{1,0:T(8,128)(2,1)} collective-permute-done((bf16[512,256]{1,0:T(8,128)(2,1)}, bf16[512,256]{1,0:T(8,128)(2,1)}, u32[]{:S(2)}, u32[]{:S(2)}) %collective-permute-start.9) | collective-permute-done | bytes 262176 | tf_op jit(solution)/shard_map/ppermute | solution.py:422
  67.3 1.2 pad_maximum_fusion.refs_0_
  68.5 2.1 %collective-permute-start.11 = (bf16[3,512,256]{2,1,0:T(8,128)(2,1)S(1)}, bf16[3,512,256]{2,1,0:T(8,128)(2,1)}, u32[]{:S(2)}, u32[]{:S(2)}) collective-permute-start(bf16[3,512,256]{2,1,0:T(8,128)(2,1)S(1)} %pad_maximum_fusion.refs_0_), channel_id=1, source_target_pairs={{0,32},{32,0},{1,33},{33,1},{2,34},{34,2},{3,35},{35,3},{4,36},{36... | collective-permute-start | bytes 2359304 | tf_op jit(solution)/shard_map/ppermute | solution.py:444
  70.6 1.1 copy-done.5
  71.7 14.2 %shard_map.87 = (bf16[2048,256]{1,0:T(8,128)(2,1)S(1)}, f32[512,1024]{1,0:T(8,128)S(1)}) custom-call(s32[25]{0:T(128)S(1)} %pad_add_fusion.place_ref, s32[128]{0:T(128)S(1)} %reshape.283.order_ref, bf16[2048,384]{1,0:T(8,128)(2,1)} %bitcast.19.refs_0_, bf16[272,1024]{1,0:T(8,128)(2,1)S(1)} %concatenate.33.refs_1_, ...), custom_call_target="tpu_custom_call" | custom-call | flops 17179869184 | bytes 8388608 | tf_op jit(solution)/shard_map/pallas_call | solution.py:281
  85.9 1.3 copy-done.2
  87.2 1.0 copy-done.3
  88.5 8.4 %all-to-all-start.1 = ((bf16[16,128,256]{2,1,0:T(8,128)(2,1)}), bf16[16,128,256]{2,1,0:T(8,128)(2,1)}, u32[]{:S(2)}, u32[]{:S(2)}) async-start(bf16[16,128,256]{2,1,0:T(8,128)(2,1)} %bitcast.48), calls=%async_computation.1 | async-start | bytes 2097152 | tf_op jit(solution)/shard_map/all_to_all | solution.py:456
  97.3 2.1 %slice.112 = bf16[256,1024]{1,0:T(8,128)(2,1)} slice(f32[512,1024]{1,0:T(8,128)} %copy-done.2), slice={[256:512], [0:1024]} | slice | bytes 1048576 | tf_op jit(solution)/shard_map/slice | solution.py:483
  99.6 14.5 %all-to-all-done.1 = bf16[16,128,256]{2,1,0:T(8,128)(2,1)} async-done(((bf16[16,128,256]{2,1,0:T(8,128)(2,1)}), bf16[16,128,256]{2,1,0:T(8,128)(2,1)}, u32[]{:S(2)}, u32[]{:S(2)}) %all-to-all-start.1) | async-done | bytes 1048608 | tf_op jit(solution)/shard_map/all_to_all | solution.py:456
  114.2 1.4 convert_reduce_fusion
  117.0 1.0 fusion.13
  119.2 1.4 convert_add_fusion
  123.8 5.2 %all-to-all-start.2 = ((bf16[8,64,256]{2,1,0:T(8,128)(2,1)}), bf16[8,64,256]{2,1,0:T(8,128)(2,1)}, u32[]{:S(2)}, u32[]{:S(2)}) async-start(bf16[8,64,256]{2,1,0:T(8,128)(2,1)} %bitcast.27), calls=%async_computation.2 | async-start | bytes 524288 | tf_op jit(solution)/shard_map/all_to_all | solution.py:475
  129.0 2.1 %constant_dynamic-slice_fusion = (bf16[2048,128]{1,0:T(8,128)(2,1)S(1)}, bf16[2048,128]{1,0:T(8,128)(2,1)}) fusion(bf16[8192,128]{1,0:T(8,128)(2,1)} %param.9, s32[]{:T(128)S(6)} %select_n.153, bf16[8192,128]{1,0:T(8,128)(2,1)} %param.8), kind=kLoop, calls=%fused_computation.63 | loop fusion | bytes 2097156 | tf_op jit(solution)/shard_map/dynamic_slice | solution.py:419
  131.1 1.8 %fusion = bf16[128,1024]{1,0:T(8,128)(2,1)} fusion(f32[128,1024]{1,0:T(8,128)} %collective-permute-done.16, f32[256,1024]{1,0:T(8,128)S(1)} %copy-done.8), kind=kLoop, calls=%fused_computation.6 | loop fusion | flops 262144 | bytes 1310720 | tf_op jit(solution)/shard_map/convert_element_type | solution.py:485
  132.9 7.2 %all-to-all-done.2 = bf16[8,64,256]{2,1,0:T(8,128)(2,1)} async-done(((bf16[8,64,256]{2,1,0:T(8,128)(2,1)}), bf16[8,64,256]{2,1,0:T(8,128)(2,1)}, u32[]{:S(2)}, u32[]{:S(2)}) %all-to-all-start.2) | async-done | bytes 262176 | tf_op jit(solution)/shard_map/all_to_all | solution.py:475
  140.1 1.2 copy.26
  141.4 1.0 copy-done.1
  142.4 3.9 %shard_map.88 = bf16[128,2048]{1,0:T(8,128)(2,1)} custom-call(s32[5]{0:T(128)S(1)} %stack.74.place_ref, bf16[128,1024]{1,0:T(8,128)(2,1)S(1)} %bitcast.47, bf16[2048,128]{1,0:T(8,128)(2,1)S(1)} %copy-done.1, bf16[2048,128]{1,0:T(8,128)(2,1)S(1)} %get-tuple-element.61.value_ref, bf16[3,512,256]{2,1,0:T(8,128)(2,1)S(1)} %pad_maximum_fusion.refs_0_, ...), custom_call_target="tpu_custom_call" | custom-call | flops 536870912 | bytes 5242880 | tf_op jit(solution)/shard_map/pallas_call | solution.py:332
  (107 shorter events, 16.0 us)
Async XLA Ops:
  0.6 1.6 %copy-start = (bf16[128,8192]{1,0:T(8,128)(2,1)S(1)}, bf16[128,8192]{1,0:T(8,128)(2,1)}, u32[]{:S(2)}) copy-start(bf16[128,8192]{1,0:T(8,128)(2,1)} %param.7) | copy-start | bytes 6291460
  2.2 2.7 %copy-start.6 = (bf16[8192,128]{1,0:T(8,128)(2,1)S(1)}, bf16[8192,128]{1,0:T(8,128)(2,1)}, u32[]{:S(2)}) copy-start(bf16[8192,128]{1,0:T(8,128)(2,1)} %param.9) | copy-start | bytes 6291460
  4.9 1.6 %copy-start.10 = (s32[128]{0:T(128)S(1)}, s32[128]{0:T(128)}, u32[]{:S(2)}) copy-start(s32[128]{0:T(128)} %param.12) | copy-start | bytes 1540
  6.2 6.0 %copy-start.9 = (bf16[128,1024]{1,0:T(8,128)(2,1)S(1)}, bf16[128,1024]{1,0:T(8,128)(2,1)}, u32[]{:S(2)}) copy-start(bf16[128,1024]{1,0:T(8,128)(2,1)} %param.10) | copy-start | bytes 786436
  6.3 3.1 %collective-permute-start.1 = (bf16[2,2,16,384]{3,2,1,0:T(8,128)(2,1)S(1)}, bf16[2,2,16,384]{3,2,1,0:T(8,128)(2,1)S(1)}, u32[]{:S(2)}, u32[]{:S(2)}) collective-permute-start(bf16[2,2,16,384]{3,2,1,0:T(8,128)(2,1)S(1)} %get-tuple-element.48), channel_id=1, source_target_pairs={{0,4},{4,0},{1,5},{5,1},{2,6},{6,2},{3,7},{7,3},{8,12},{12,8},{9,1... | collective-permute-start | bytes 147464 | tf_op jit(solution)/shard_map/ppermute | solution.py:385
  9.5 4.3 %collective-permute-start.2 = (bf16[2,2,16,384]{3,2,1,0:T(8,128)(2,1)S(1)}, bf16[2,2,16,384]{3,2,1,0:T(8,128)(2,1)S(1)}, u32[]{:S(2)}, u32[]{:S(2)}) collective-permute-start(bf16[2,2,16,384]{3,2,1,0:T(8,128)(2,1)S(1)} %get-tuple-element.47), channel_id=1, source_target_pairs={{0,32},{32,0},{1,33},{33,1},{2,34},{34,2},{3,35},{35,3},{4,36},{36... | collective-permute-start | bytes 147464 | tf_op jit(solution)/shard_map/ppermute | solution.py:387
  15.2 32.1 %all-to-all-start = ((bf16[16,128,384]{2,1,0:T(8,128)(2,1)}), bf16[16,128,384]{2,1,0:T(8,128)(2,1)}, u32[]{:S(2)}, u32[]{:S(2)}) async-start(bf16[16,128,384]{2,1,0:T(8,128)(2,1)} %broadcast_in_dim.16), calls=%async_computation | async-start | bytes 3145728 | tf_op jit(solution)/shard_map/all_to_all | solution.py:425
  22.2 13.6 %collective-permute-start.3 = (bf16[272,1024]{1,0:T(8,128)(2,1)S(1)}, bf16[272,1024]{1,0:T(8,128)(2,1)S(1)}, u32[]{:S(2)}, u32[]{:S(2)}) collective-permute-start(bf16[272,1024]{1,0:T(8,128)(2,1)S(1)} %concatenate.33.refs_1_), channel_id=1, source_target_pairs={{0,32},{32,0},{1,33},{33,1},{2,34},{34,2},{3,35},{35,3},{4,36},{36... | collective-permute-start | bytes 1671176 | tf_op jit(solution)/shard_map/ppermute | solution.py:399
  22.5 22.8 %collective-permute-start = (bf16[272,1024]{1,0:T(8,128)(2,1)S(1)}, bf16[272,1024]{1,0:T(8,128)(2,1)}, u32[]{:S(2)}, u32[]{:S(2)}) collective-permute-start(bf16[272,1024]{1,0:T(8,128)(2,1)S(1)} %concatenate.33.refs_1_), channel_id=1, source_target_pairs={{0,4},{4,0},{1,5},{5,1},{2,6},{6,2},{3,7},{7,3},{8,12},{12,8},{9,1... | collective-permute-start | bytes 1671176 | tf_op jit(solution)/shard_map/ppermute | solution.py:402
  35.8 20.5 %copy-start.4 = (bf16[272,1024]{1,0:T(8,128)(2,1)}, bf16[272,1024]{1,0:T(8,128)(2,1)S(1)}, u32[]{:S(2)}) copy-start(bf16[272,1024]{1,0:T(8,128)(2,1)S(1)} %collective-permute-done.3.refs_3_) | copy-start | bytes 1671172
  35.8 10.5 %collective-permute-start.4 = (bf16[272,1024]{1,0:T(8,128)(2,1)S(1)}, bf16[272,1024]{1,0:T(8,128)(2,1)}, u32[]{:S(2)}, u32[]{:S(2)}) collective-permute-start(bf16[272,1024]{1,0:T(8,128)(2,1)S(1)} %collective-permute-done.3.refs_3_), channel_id=1, source_target_pairs={{0,4},{4,0},{1,5},{5,1},{2,6},{6,2},{3,7},{7,3},{8,12},{12,8},{9,1... | collective-permute-start | bytes 1671176 | tf_op jit(solution)/shard_map/ppermute | solution.py:404
  36.1 21.8 %collective-permute-start.10 = (bf16[512,256]{1,0:T(8,128)(2,1)}, bf16[512,256]{1,0:T(8,128)(2,1)}, u32[]{:S(2)}, u32[]{:S(2)}) collective-permute-start(bf16[512,256]{1,0:T(8,128)(2,1)} %pad_maximum_fusion.3), channel_id=1, source_target_pairs={{0,3},{1,0},{2,1},{3,2},{4,7},{5,4},{6,5},{7,6},{8,11},{9,8},{10,9... | collective-permute-start | bytes 786440 | tf_op jit(solution)/shard_map/ppermute | solution.py:422
  41.6 22.8 %collective-permute-start.8 = (bf16[512,256]{1,0:T(8,128)(2,1)}, bf16[512,256]{1,0:T(8,128)(2,1)}, u32[]{:S(2)}, u32[]{:S(2)}) collective-permute-start(bf16[512,256]{1,0:T(8,128)(2,1)} %pad_maximum_fusion.1), channel_id=1, source_target_pairs={{0,1},{1,2},{2,3},{3,0},{4,5},{5,6},{6,7},{7,4},{8,9},{9,10},{10,1... | collective-permute-start | bytes 786440 | tf_op jit(solution)/shard_map/ppermute | solution.py:422
  41.6 25.7 %collective-permute-start.9 = (bf16[512,256]{1,0:T(8,128)(2,1)}, bf16[512,256]{1,0:T(8,128)(2,1)}, u32[]{:S(2)}, u32[]{:S(2)}) collective-permute-start(bf16[512,256]{1,0:T(8,128)(2,1)} %pad_maximum_fusion.2), channel_id=1, source_target_pairs={{0,2},{1,3},{2,0},{3,1},{4,6},{5,7},{6,4},{7,5},{8,10},{9,11},{10,... | collective-permute-start | bytes 786440 | tf_op jit(solution)/shard_map/ppermute | solution.py:422
  56.3 11.0 %collective-permute-start.5 = (f32[16,512]{1,0:T(8,128)S(1)}, f32[16,512]{1,0:T(8,128)S(1)}, u32[]{:S(2)}, u32[]{:S(2)}) collective-permute-start(f32[16,512]{1,0:T(8,128)S(1)} %shard_map.86.refs_5_), channel_id=1, source_target_pairs={{0,4},{4,0},{1,5},{5,1},{2,6},{6,2},{3,7},{7,3},{8,12},{12,8},{9,1... | collective-permute-start | bytes 98312 | tf_op jit(solution)/shard_map/ppermute | solution.py:438
  56.4 10.9 %collective-permute-start.6 = (f32[16,512]{1,0:T(8,128)S(1)}, f32[16,512]{1,0:T(8,128)S(1)}, u32[]{:S(2)}, u32[]{:S(2)}) collective-permute-start(f32[16,512]{1,0:T(8,128)S(1)} %shard_map.86.refs_5_), channel_id=1, source_target_pairs={{0,32},{32,0},{1,33},{33,1},{2,34},{34,2},{3,35},{35,3},{4,36},{36... | collective-permute-start | bytes 98312 | tf_op jit(solution)/shard_map/ppermute | solution.py:439
  57.9 9.4 %collective-permute-start.7 = (f32[16,512]{1,0:T(8,128)S(1)}, f32[16,512]{1,0:T(8,128)S(1)}, u32[]{:S(2)}, u32[]{:S(2)}) collective-permute-start(f32[16,512]{1,0:T(8,128)S(1)} %shard_map.86.refs_5_), channel_id=1, source_target_pairs={{0,36},{4,32},{32,4},{36,0},{1,37},{5,33},{33,5},{37,1},{2,38},{6,... | collective-permute-start | bytes 98312 | tf_op jit(solution)/shard_map/ppermute | solution.py:440
  68.5 20.0 %collective-permute-start.11 = (bf16[3,512,256]{2,1,0:T(8,128)(2,1)S(1)}, bf16[3,512,256]{2,1,0:T(8,128)(2,1)}, u32[]{:S(2)}, u32[]{:S(2)}) collective-permute-start(bf16[3,512,256]{2,1,0:T(8,128)(2,1)S(1)} %pad_maximum_fusion.refs_0_), channel_id=1, source_target_pairs={{0,32},{32,0},{1,33},{33,1},{2,34},{34,2},{3,35},{35,3},{4,36},{36... | collective-permute-start | bytes 2359304 | tf_op jit(solution)/shard_map/ppermute | solution.py:444
  70.6 1.1 copy-start.5
  85.9 1.3 copy-start.2
  87.2 1.0 copy-start.3
  88.5 25.6 %all-to-all-start.1 = ((bf16[16,128,256]{2,1,0:T(8,128)(2,1)}), bf16[16,128,256]{2,1,0:T(8,128)(2,1)}, u32[]{:S(2)}, u32[]{:S(2)}) async-start(bf16[16,128,256]{2,1,0:T(8,128)(2,1)} %bitcast.48), calls=%async_computation.1 | async-start | bytes 2097152 | tf_op jit(solution)/shard_map/all_to_all | solution.py:456
  97.2 44.1 %collective-permute-start.13 = (bf16[3,512,256]{2,1,0:T(8,128)(2,1)S(1)}, bf16[3,512,256]{2,1,0:T(8,128)(2,1)}, u32[]{:S(2)}, u32[]{:S(2)}) collective-permute-start(bf16[3,512,256]{2,1,0:T(8,128)(2,1)S(1)} %pad_maximum_fusion.refs_0_), channel_id=1, source_target_pairs={{0,4},{4,0},{1,5},{5,1},{2,6},{6,2},{3,7},{7,3},{8,12},{12,8},{9,1... | collective-permute-start | bytes 2359304 | tf_op jit(solution)/shard_map/ppermute | solution.py:452
  99.4 19.9 %collective-permute-start.15 = (bf16[256,1024]{1,0:T(8,128)(2,1)}, bf16[256,1024]{1,0:T(8,128)(2,1)S(1)}, u32[]{:S(2)}, u32[]{:S(2)}) collective-permute-start(bf16[256,1024]{1,0:T(8,128)(2,1)} %slice.112), channel_id=1, source_target_pairs={{0,32},{32,0},{1,33},{33,1},{2,34},{34,2},{3,35},{35,3},{4,36},{36... | collective-permute-start | bytes 1572872 | tf_op jit(solution)/shard_map/ppermute | solution.py:483
  119.1 3.8 %collective-permute-start.12 = (bf16[2,2,16,256]{3,2,1,0:T(8,128)(2,1)S(1)}, bf16[2,2,16,256]{3,2,1,0:T(8,128)(2,1)S(1)}, u32[]{:S(2)}, u32[]{:S(2)}) collective-permute-start(bf16[2,2,16,256]{3,2,1,0:T(8,128)(2,1)S(1)} %get-tuple-element.55), channel_id=1, source_target_pairs={{0,4},{4,0},{1,5},{5,1},{2,6},{6,2},{3,7},{7,3},{8,12},{12,8},{9,1... | collective-permute-start | bytes 98312 | tf_op jit(solution)/shard_map/ppermute | solution.py:470
  120.6 1.0 copy-start.7
  122.4 8.7 %collective-permute-start.16 = (f32[128,1024]{1,0:T(8,128)}, f32[128,1024]{1,0:T(8,128)}, u32[]{:S(2)}, u32[]{:S(2)}) collective-permute-start(f32[128,1024]{1,0:T(8,128)} %slice.90), channel_id=1, source_target_pairs={{0,4},{4,0},{1,5},{5,1},{2,6},{6,2},{3,7},{7,3},{8,12},{12,8},{9,1... | collective-permute-start | bytes 1572872 | tf_op jit(solution)/shard_map/ppermute | solution.py:484
  122.9 18.4 %collective-permute-start.14 = (bf16[3,512,256]{2,1,0:T(8,128)(2,1)}, bf16[3,512,256]{2,1,0:T(8,128)(2,1)}, u32[]{:S(2)}, u32[]{:S(2)}) collective-permute-start(bf16[3,512,256]{2,1,0:T(8,128)(2,1)} %collective-permute-done.11.refs_1_), channel_id=1, source_target_pairs={{0,4},{4,0},{1,5},{5,1},{2,6},{6,2},{3,7},{7,3},{8,12},{12,8},{9,1... | collective-permute-start | bytes 2359304 | tf_op jit(solution)/shard_map/ppermute | solution.py:453
  123.8 16.4 %all-to-all-start.2 = ((bf16[8,64,256]{2,1,0:T(8,128)(2,1)}), bf16[8,64,256]{2,1,0:T(8,128)(2,1)}, u32[]{:S(2)}, u32[]{:S(2)}) async-start(bf16[8,64,256]{2,1,0:T(8,128)(2,1)} %bitcast.27), calls=%async_computation.2 | async-start | bytes 524288 | tf_op jit(solution)/shard_map/all_to_all | solution.py:475
  129.0 2.2 %copy-start.8 = (f32[256,1024]{1,0:T(8,128)S(1)}, f32[256,1024]{1,0:T(8,128)}, u32[]{:S(2)}) copy-start(f32[256,1024]{1,0:T(8,128)} %copy-done.7) | copy-start | bytes 3145732
  141.4 1.0 copy-start.1
